TPU v7x, 768 devices: a whole 4x8x12 slice. The times are simulated.
768 devices in a mesh: ep: 64 (over x, y, z_hi), dp: 12 (over z_lo, core).
Axes of the slice: x: 4, y: 8, z: 12 (z_hi: 2, z_lo: 6; z = z_hi * 6 + z_lo), core: 2. Of those that a mesh axis runs over, the one named last changes fastest.
Arguments:
- out_grad: bfloat16 [1024, 2048], P('ep'), may hold values from -6 to 6
- route_probs: float32 [1024, 8], P('ep'), may hold values from 0.02 to 0.3
- routes: int32 [1024, 8], P('ep'), may hold values from 0 to 127, all different within a row; in each aligned block of 16 rows (0 to 15, 16 to 31, ...) at most 2 rows name the same one
- replica_expert: int32 [64], replicated, may hold values from 0 to 63, as said below
- saved_inputs: bfloat16 [64, 2, 64, 2, 2048], P('ep'), may hold values from -6 to 6
- home_gate_up: bfloat16 [64, 2, 2048, 1536], P('ep', None, None, 'dp'), may hold values from -1 to 1
- home_down: bfloat16 [64, 1536, 2048], P('ep', 'dp'), may hold values from -1 to 1
- replica_gate_up: bfloat16 [64, 2, 2048, 1536], P('ep', None, None, 'dp'), may hold values from -1 to 1, as said below
- replica_down: bfloat16 [64, 1536, 2048], P('ep', 'dp'), may hold values from -1 to 1, as said below
Outputs:
- input_grad: bfloat16 [1024, 2048], P('ep')
- grad_gate_up: bfloat16 [64, 2, 2048, 1536], P('ep', None, None, 'dp')
- grad_down: bfloat16 [64, 1536, 2048], P('ep', 'dp')
Inputs may be any that keep to these rules, and one draw needn't show every extreme that they name: `routes`: each token names 8 different slots; slot s lies at index s // 2 of ep as its slot s % 2. Among the tokens of one index of ep no slot is named more than 2 times, a bound that some block reaches. `replica_expert`: entry c is c or c + 1; the last entry is 63. replica_gate_up[c] equals home_gate_up[replica_expert[c]]. replica_down[c] equals home_down[replica_expert[c]].
All inputs are finite; a program needn't handle non-finite values.
Results may differ from a plain program's by a relative error of at most 0.022.
Values may be sent and summed in bfloat16 or wider, within the bound.
No kernel may reach another device: no remote copies, remote signals or barrier semaphores. Data moves between devices by JAX's collectives and lax.ppermute only.
A program may use at most 64 MiB of HBM per device.

v0:
```python
import jax
import jax.numpy as jnp
from jax import lax
from jax.sharding import PartitionSpec as P


def passed_along(array, axis, by):
    length = lax.axis_size(axis)
    pairs = [(i, i + by) for i in range(length) if 0 <= i + by < length]
    return lax.ppermute(array, axis, pairs)


def slot_backward(inputs, block_grad, gate_up, down_weight):
    gate_pre = jnp.dot(inputs, gate_up[0], preferred_element_type=jnp.float32)
    up_pre = jnp.dot(inputs, gate_up[1], preferred_element_type=jnp.float32)
    sigmoid_gate = jax.nn.sigmoid(gate_pre)
    active = gate_pre * sigmoid_gate
    hidden = (active * up_pre).astype(jnp.bfloat16)
    contract_cols = (((1,), (1,)), ((), ()))
    rows_first = (((0,), (0,)), ((), ()))
    hidden_grad = lax.dot_general(
        block_grad, down_weight, contract_cols, preferred_element_type=jnp.float32
    )
    up_grad = (hidden_grad * active).astype(jnp.bfloat16)
    gate_grad = (
        hidden_grad * up_pre * sigmoid_gate * (1.0 + gate_pre * (1.0 - sigmoid_gate))
    ).astype(jnp.bfloat16)
    weight_gate = lax.dot_general(inputs, gate_grad, rows_first, preferred_element_type=jnp.float32)
    weight_up = lax.dot_general(inputs, up_grad, rows_first, preferred_element_type=jnp.float32)
    weight_down = lax.dot_general(
        hidden, block_grad, rows_first, preferred_element_type=jnp.float32
    )
    partial_rows = lax.dot_general(
        gate_grad, gate_up[0], contract_cols, preferred_element_type=jnp.float32
    )
    partial_rows = partial_rows + lax.dot_general(
        up_grad, gate_up[1], contract_cols, preferred_element_type=jnp.float32
    )
    return (partial_rows.astype(jnp.bfloat16), (weight_gate, weight_up, weight_down))


def on_device(
    out_grad,
    route_probs,
    routes,
    replica_expert,
    saved_inputs,
    home_gate_up,
    home_down,
    replica_gate_up,
    replica_down,
):
    holders = lax.axis_size("ep")
    token_count, top_count = routes.shape
    model_width = out_grad.shape[1]
    capacity = saved_inputs.shape[3]
    block_rows = holders * capacity
    route_slots = routes.reshape(-1)
    slot_ids = lax.iota(jnp.int32, 2 * holders)
    matches = (route_slots[:, None] == slot_ids[None, :]).astype(jnp.int32)
    earlier_count = jnp.cumsum(matches, axis=0) - matches
    position = jnp.sum(earlier_count * matches, axis=1)
    target_row = route_slots % 2 * block_rows + route_slots // 2 * capacity + position
    row_ids = lax.iota(jnp.int32, 2 * block_rows)
    placement_table = (target_row[:, None] == row_ids[None, :]).astype(jnp.bfloat16)
    routed_grad = (
        (route_probs[:, :, None] * out_grad[:, None, :].astype(jnp.float32))
        .reshape(-1, model_width)
        .astype(jnp.bfloat16)
    )
    outgoing = jnp.einsum(
        "rb,rd->bd", placement_table, routed_grad, preferred_element_type=jnp.float32
    ).astype(jnp.bfloat16)
    outgoing = outgoing.reshape(2, holders, capacity, model_width)
    incoming = lax.all_to_all(outgoing, "ep", split_axis=1, concat_axis=1, tiled=True)
    block_grad = incoming.reshape(2, block_rows, model_width)
    held_inputs = saved_inputs.reshape(2, block_rows, model_width)
    column = lax.axis_index("ep")
    own_entry = replica_expert[column]
    prior_entry = replica_expert[jnp.maximum(column - 1, 0)]
    keeps_own = own_entry == column
    takes_prior = (column > 0) & (prior_entry == column)
    home_rows, home_weights = slot_backward(
        held_inputs[0], block_grad[0], home_gate_up[0], home_down[0]
    )
    spare_rows, spare_weights = slot_backward(
        held_inputs[1], block_grad[1], replica_gate_up[0], replica_down[0]
    )
    width_rows, unit_cols = spare_weights[0].shape
    packed = jnp.stack(
        [spare_weights[0], spare_weights[1], spare_weights[2].reshape(width_rows, unit_cols)]
    )
    received = passed_along(packed, "ep", 1)
    received_parts = (received[0], received[1], received[2].reshape(unit_cols, width_rows))
    totals = [
        home_part + jnp.where(keeps_own, spare_part, 0.0) + jnp.where(takes_prior, prior_part, 0.0)
        for home_part, spare_part, prior_part in zip(home_weights, spare_weights, received_parts)
    ]
    partial_rows = jnp.stack([home_rows, spare_rows])
    grad_gate_up = jnp.stack([totals[0], totals[1]])[None].astype(jnp.bfloat16)
    grad_down = totals[2][None].astype(jnp.bfloat16)
    block_total = lax.psum(partial_rows.astype(jnp.float32).astype(jnp.bfloat16), "dp")
    returned = lax.all_to_all(
        block_total.reshape(2, holders, capacity, model_width),
        "ep",
        split_axis=1,
        concat_axis=1,
        tiled=True,
    )
    route_rows = jnp.einsum(
        "rb,bd->rd",
        placement_table,
        returned.reshape(2 * block_rows, model_width),
        preferred_element_type=jnp.float32,
    )
    input_grad = jnp.sum(route_rows.reshape(token_count, top_count, model_width), axis=1).astype(
        jnp.bfloat16
    )
    return (input_grad, grad_gate_up, grad_down)


def solution(mesh):
    placed = (
        P("ep", None),
        P("ep", None),
        P("ep", None),
        P(),
        P("ep", None, None, None, None),
        P("ep", None, None, "dp"),
        P("ep", "dp", None),
        P("ep", None, None, "dp"),
        P("ep", "dp", None),
    )
    return jax.shard_map(
        on_device,
        mesh=mesh,
        in_specs=placed,
        out_specs=(P("ep", None), P("ep", None, None, "dp"), P("ep", "dp", None)),
        check_vma=False,
    )
```

profile of v0, /device:TPU:1, one launch (start us, length us, event | category | flops | bytes accessed | tf_op | source)
XLA Modules:
  0.0 438.8 jit_solution(7100467596455387455)
XLA Ops:
  7.2 0.8 copy.28
  9.4 0.9 convert_element_type.59
  11.5 2.2 copy.34
  13.7 24.1 %all-to-all-start = ((bf16[2,64,2,2048]{3,2,0,1:T(2,128)(2,1)}), bf16[2,64,2,2048]{3,2,0,1:T(2,128)(2,1)}, u32[]{:S(2)}, u32[]{:S(2)}) async-start(bf16[2,64,2,2048]{3,2,0,1:T(2,128)(2,1)} %copy.34), calls=%async_computation | async-start | bytes 2097152 | tf_op jit(solution)/shard_map/all_to_all | solution.py:75
  37.9 2.0 fusion.69
  40.3 1.3 fusion.28
  41.6 1.3 fusion.31
  43.5 19.1 %all-to-all-done = bf16[2,64,2,2048]{3,2,0,1:T(2,128)(2,1)} async-done(((bf16[2,64,2,2048]{3,2,0,1:T(2,128)(2,1)}), bf16[2,64,2,2048]{3,2,0,1:T(2,128)(2,1)}, u32[]{:S(2)}, u32[]{:S(2)}) %all-to-all-start) | async-done | bytes 1048608 | tf_op jit(solution)/shard_map/all_to_all | solution.py:75
  62.6 2.7 fusion.68
  65.6 1.3 fusion.52
  67.5 2.3 fusion.17
  69.8 1.2 squeeze.44
  71.1 2.6 stack_reshape.3
  73.6 2.6 copy.37
  76.6 3.6 pad_maximum_fusion
  80.2 13.2 %collective-permute-start = (f32[3,2048,128]{1,2,0:T(8,128)}, f32[3,2048,128]{1,2,0:T(8,128)}, u32[]{:S(2)}, u32[]{:S(2)}) collective-permute-start(f32[3,2048,128]{1,2,0:T(8,128)} %pad_maximum_fusion), channel_id=1, source_target_pairs={{0,12},{12,24},{24,36},{36,48},{48,60},{60,72},{72,84},{84,96},{96... | collective-permute-start | bytes 9437192 | tf_op jit(solution)/shard_map/ppermute | solution.py:10
  94.8 1.5 reshape.166
  96.3 3.6 copy.35
  99.9 276.0 %all-reduce.2.cloned.1.call-done = bf16[2,64,2,2048]{3,2,0,1:T(2,128)(2,1)} async-done(((bf16[2,64,2,2048]{3,2,0,1:T(2,128)(2,1)}), bf16[2,64,2,2048]{3,2,0,1:T(2,128)(2,1)}) %all-reduce.2.cloned.1.call-update) | async-done | bytes 1048592 | tf_op jit(solution)/shard_map/psum | solution.py:102
  375.9 13.3 %all-to-all-start.1 = ((bf16[2,64,2,2048]{3,2,0,1:T(2,128)(2,1)}), bf16[2,64,2,2048]{3,2,0,1:T(2,128)(2,1)}, u32[]{:S(2)}, u32[]{:S(2)}) async-start(bf16[2,64,2,2048]{3,2,0,1:T(2,128)(2,1)} %all-reduce.2.cloned.1.call-done), calls=%async_computation.1 | async-start | bytes 2097152 | tf_op jit(solution)/shard_map/all_to_all | solution.py:103
  391.2 2.4 convolution_add_fusion
  393.6 2.4 slice_select_fusion
  396.0 2.5 copy.38
  398.5 2.4 select_n.89
  400.9 1.6 fusion.12
  402.5 1.7 fusion.13
  404.2 1.2 pad_maximum_fusion.2
  405.3 2.3 copy.39
  407.6 0.9 fusion.15
  408.5 19.9 %all-to-all-done.1 = bf16[2,64,2,2048]{3,2,0,1:T(2,128)(2,1)} async-done(((bf16[2,64,2,2048]{3,2,0,1:T(2,128)(2,1)}), bf16[2,64,2,2048]{3,2,0,1:T(2,128)(2,1)}, u32[]{:S(2)}, u32[]{:S(2)}) %all-to-all-start.1) | async-done | bytes 1048608 | tf_op jit(solution)/shard_map/all_to_all | solution.py:103
  428.4 1.9 copy.36
  430.8 1.1 convolution_reduce_fusion
  (55 shorter events, 7.3 us)
Async XLA Ops:
  7.2 59.7 %copy-start = (bf16[1,128,2048]{2,1,0:T(8,128)(2,1)S(1)}, bf16[1,128,2048]{2,1,0:T(8,128)(2,1)}, u32[]{:S(2)}) copy-start(bf16[1,128,2048]{2,1,0:T(8,128)(2,1)} %param.17) | copy-start | bytes 1572868
  13.7 48.9 %all-to-all-start = ((bf16[2,64,2,2048]{3,2,0,1:T(2,128)(2,1)}), bf16[2,64,2,2048]{3,2,0,1:T(2,128)(2,1)}, u32[]{:S(2)}, u32[]{:S(2)}) async-start(bf16[2,64,2,2048]{3,2,0,1:T(2,128)(2,1)} %copy.34), calls=%async_computation | async-start | bytes 2097152 | tf_op jit(solution)/shard_map/all_to_all | solution.py:75
  37.8 5.1 %copy-start.4 = (bf16[1,2,2048,128]{3,2,1,0:T(8,128)(2,1)S(1)}, bf16[1,2,2048,128]{3,2,1,0:T(8,128)(2,1)}, u32[]{:S(2)}) copy-start(bf16[1,2,2048,128]{3,2,1,0:T(8,128)(2,1)} %param.16) | copy-start | bytes 3145732
  37.8 338.1 %all-reduce.2.cloned.1.call-start = ((), (), s32[]{:S(2)}) async-start(), calls=%async_computation.2 | async-start | bytes 2097152 | tf_op jit(solution)/shard_map/psum | solution.py:102
  71.0 22.4 %copy-start.10 = (bf16[128,2048]{1,0:T(8,128)(2,1)}, bf16[128,2048]{1,0:T(8,128)(2,1)S(1)}, u32[]{:S(2)}) copy-start(bf16[128,2048]{1,0:T(8,128)(2,1)S(1)} %squeeze.44) | copy-start | bytes 1572868
  76.5 3.6 copy-start.2
  76.5 16.9 %copy-start.12 = (bf16[1,128,2048]{2,1,0:T(8,128)(2,1)S(1)}, bf16[1,128,2048]{2,1,0:T(8,128)(2,1)}, u32[]{:S(2)}) copy-start(bf16[1,128,2048]{2,1,0:T(8,128)(2,1)} %param.15) | copy-start | bytes 1572868
  76.6 17.2 %copy-start.5 = (bf16[1,2,2048,128]{3,2,1,0:T(8,128)(2,1)S(1)}, bf16[1,2,2048,128]{3,2,1,0:T(8,128)(2,1)}, u32[]{:S(2)}) copy-start(bf16[1,2,2048,128]{3,2,1,0:T(8,128)(2,1)} %param.16) | copy-start | bytes 3145732
  76.6 17.2 %copy-start.8 = (f32[128,2048]{1,0:T(8,128)S(1)}, f32[128,2048]{1,0:T(8,128)}, u32[]{:S(2)}) copy-start(f32[128,2048]{1,0:T(8,128)} %fusion.17) | copy-start | bytes 3145732
  80.2 13.9 %copy-start.6 = (bf16[1,2,2048,128]{3,2,1,0:T(8,128)(2,1)S(1)}, bf16[1,2,2048,128]{3,2,1,0:T(8,128)(2,1)}, u32[]{:S(2)}) copy-start(bf16[1,2,2048,128]{3,2,1,0:T(8,128)(2,1)} %param.14) | copy-start | bytes 3145732
  80.2 313.4 %collective-permute-start = (f32[3,2048,128]{1,2,0:T(8,128)}, f32[3,2048,128]{1,2,0:T(8,128)}, u32[]{:S(2)}, u32[]{:S(2)}) collective-permute-start(f32[3,2048,128]{1,2,0:T(8,128)} %pad_maximum_fusion), channel_id=1, source_target_pairs={{0,12},{12,24},{24,36},{36,48},{48,60},{60,72},{72,84},{84,96},{96... | collective-permute-start | bytes 9437192 | tf_op jit(solution)/shard_map/ppermute | solution.py:10
  96.3 293.0 %copy-start.11 = (s32[64]{0:T(128)S(1)}, s32[64]{0:T(128)}, u32[]{:S(2)}) copy-start(s32[64]{0:T(128)} %param.12) | copy-start | bytes 772
  96.3 294.9 %copy-start.1 = (f32[128,2048]{1,0:T(8,128)S(1)}, f32[128,2048]{1,0:T(8,128)}, u32[]{:S(2)}) copy-start(f32[128,2048]{1,0:T(8,128)} %fusion.52) | copy-start | bytes 3145732
  375.9 52.5 %all-to-all-start.1 = ((bf16[2,64,2,2048]{3,2,0,1:T(2,128)(2,1)}), bf16[2,64,2,2048]{3,2,0,1:T(2,128)(2,1)}, u32[]{:S(2)}, u32[]{:S(2)}) async-start(bf16[2,64,2,2048]{3,2,0,1:T(2,128)(2,1)} %all-reduce.2.cloned.1.call-done), calls=%async_computation.1 | async-start | bytes 2097152 | tf_op jit(solution)/shard_map/all_to_all | solution.py:103
  393.6 7.3 %copy-start.3 = (f32[128,2048]{1,0:T(8,128)S(1)}, f32[128,2048]{1,0:T(8,128)}, u32[]{:S(2)}) copy-start(f32[128,2048]{1,0:T(8,128)} %copy-done.2) | copy-start | bytes 3145732
  402.5 5.1 %copy-start.7 = (f32[128,2048]{1,0:T(8,128)S(1)}, f32[128,2048]{1,0:T(8,128)}, u32[]{:S(2)}) copy-start(f32[128,2048]{1,0:T(8,128)} %convolution_add_fusion) | copy-start | bytes 3145732
  404.1 3.4 copy-start.9
Sparse Core Ops, SparseCore 0:
  100.0 275.8 all-reduce.1
where the time goes:
time: 440 us; the launch traced here: 439 us
  waiting for transfers between devices  315 us (72%)
  starting transfers between devices  50.6 us (12%)
  local copies, waits for them, and re-layouts  31.7 us (7%)
  matrix products  16.2 us (4%)
  between operations  15.7 us (4%)
  other arithmetic  9.45 us (2%)
    psum x1, waiting for transfers between devices, on_device(): lax.psum(partial_rows.astype(jnp.float32).astype(jnp.bfloat16), 'dp')  276 us
    all_to_all x1, starting transfers between devices, on_device(): lax.all_to_all(outgoing, 'ep', split_axis=1, concat_axis=1, tiled=True)  24.1 us
    all_to_all x1, waiting for transfers between devices, on_device(): lax.all_to_all(block_total.reshape(2, holders, capacity, model_width), 'e...  19.9 us
    all_to_all x1, waiting for transfers between devices, on_device(): lax.all_to_all(outgoing, 'ep', split_axis=1, concat_axis=1, tiled=True)  19.1 us
    all_to_all x1, starting transfers between devices, on_device(): lax.all_to_all(block_total.reshape(2, holders, capacity, model_width), 'e...  13.3 us
    ppermute x1, starting transfers between devices, passed_along(): return lax.ppermute(array, axis, pairs)  13.2 us
  transfers between devices with their start and end apart: 4, of which 3 were waited for; matrix products, arithmetic and copies ran while one was open for 7% of the time, Pallas kernels for 0%

commit v1 on v0

v1 whole, which is shorter than its diff:
```python
import jax
import jax.numpy as jnp
from jax import lax
from jax.sharding import PartitionSpec as P

BF = jnp.bfloat16
F32 = jnp.float32
COLS = (((1,), (1,)), ((), ()))
ROWS = (((0,), (0,)), ((), ()))


def along_dp(array, to):
    pairs = [(2 * z + c, 2 * to(z)[0] + (c ^ to(z)[1])) for z in range(6) for c in range(2)]
    return lax.ppermute(array, "dp", pairs)


def swap_cores(array):
    return along_dp(array, lambda z: (z, 1))


def to_next(array):
    length = lax.axis_size("ep")
    return lax.ppermute(array, "ep", [(i, i + 1) for i in range(length - 1)])


def exchange(array):
    return lax.all_to_all(array, "ep", split_axis=0, concat_axis=0, tiled=True)


def joined(own, other, core):
    first = jnp.where(core == 0, own, other)
    second = jnp.where(core == 0, other, own)
    return jnp.concatenate([first, second], axis=-1)


def act(x, gate_up):
    gate = jnp.dot(x, gate_up[0], preferred_element_type=F32)
    up = jnp.dot(x, gate_up[1], preferred_element_type=F32)
    sig = jax.nn.sigmoid(gate)
    active = gate * sig
    hidden = (active * up).astype(BF)
    slope = up * sig * (1.0 + gate * (1.0 - sig))
    return active, slope, hidden


def hidden_grads(block, down, active, slope):
    hg = lax.dot_general(block, down, COLS, preferred_element_type=F32)
    return (hg * slope).astype(BF), (hg * active).astype(BF)


def on_device(
    out_grad,
    route_probs,
    routes,
    replica_expert,
    saved_inputs,
    home_gate_up,
    home_down,
    replica_gate_up,
    replica_down,
):
    n_ep = lax.axis_size("ep")
    tokens, top = routes.shape
    width = out_grad.shape[1]
    half = width // 2
    cap = saved_inputs.shape[3]
    rows = n_ep * cap
    column = lax.axis_index("ep")
    core = lax.axis_index("dp") % 2

    spare_half = lax.dynamic_slice_in_dim(saved_inputs[0, 1], core * half, half, 2)
    prior_x_own = to_next(spare_half)

    slot_ids = lax.iota(jnp.int32, 2 * n_ep)
    names = routes[:, :, None] == slot_ids[None, None, :]
    named = jnp.any(names, axis=1)
    prob_ts = jnp.sum(jnp.where(names, route_probs[:, :, None], 0.0), axis=1)
    earlier = jnp.cumsum(named.astype(jnp.int32), axis=0) - named.astype(jnp.int32)
    place = jnp.stack([named & (earlier == p) for p in range(cap)])
    row_prob = jnp.sum(jnp.where(place, prob_ts[None], 0.0), axis=1)
    table = place.astype(BF).transpose(2, 0, 1).reshape(n_ep * 2 * cap, tokens)
    row_prob = row_prob.T.reshape(n_ep * 2 * cap, 1)
    out_half = lax.dynamic_slice_in_dim(out_grad, core * half, half, 1)
    outgoing = (jnp.dot(table, out_half, preferred_element_type=F32) * row_prob).astype(BF)
    incoming = exchange(outgoing.reshape(n_ep, 16, half // 4))

    held = saved_inputs.reshape(2, rows, width)
    home_act = act(held[0], home_gate_up[0])
    spare_act = act(held[1], replica_gate_up[0])
    prior_x = joined(prior_x_own, swap_cores(prior_x_own), core).reshape(rows, width)
    prior_act = act(prior_x, home_gate_up[0])

    other_in = swap_cores(incoming)
    block = joined(
        incoming.reshape(n_ep, 2 * cap, half), other_in.reshape(n_ep, 2 * cap, half), core
    )
    block = block.reshape(n_ep, 2, cap, width)
    block_home = block[:, 0].reshape(rows, width)
    block_spare = block[:, 1].reshape(rows, width)
    gg_home, ug_home = hidden_grads(block_home, home_down[0], home_act[0], home_act[1])
    gg_spare, ug_spare = hidden_grads(block_spare, replica_down[0], spare_act[0], spare_act[1])

    def back(start):
        parts = []
        for gg, ug, w in ((gg_home, ug_home, home_gate_up[0]), (gg_spare, ug_spare, replica_gate_up[0])):
            wg = lax.dynamic_slice_in_dim(w, start, half, 1)
            part = lax.dot_general(gg, wg[0], COLS, preferred_element_type=F32)
            parts.append(part + lax.dot_general(ug, wg[1], COLS, preferred_element_type=F32))
        return jnp.stack([p.reshape(n_ep, cap, half) for p in parts], axis=1)

    sent = back((1 - core) * half).astype(BF).reshape(n_ep, 16, half // 4)
    kept = back(core * half)
    pair_sum = kept.reshape(n_ep, 16, half // 4) + swap_cores(sent).astype(F32)
    returned = exchange(pair_sum.astype(BF))

    back_table = table.reshape(n_ep * 2 * cap, tokens)
    mine = lax.dot_general(
        back_table, returned.reshape(n_ep * 2 * cap, half), ROWS, preferred_element_type=F32
    )
    total = mine + along_dp(mine.astype(BF), lambda z: (z ^ 1, 0)).astype(F32)
    low = total.astype(BF)
    one = along_dp(low, lambda z: ((z + 2) % 6, 0))
    two = along_dp(low, lambda z: ((z + 4) % 6, 0))
    total = (total + one.astype(F32) + two.astype(F32)).astype(BF)
    input_grad = joined(total, swap_cores(total), core)

    prior_own = to_next(incoming.reshape(n_ep, 2, 8, half // 4)[:, 1])
    prior_block = joined(
        prior_own.reshape(n_ep, cap, half), swap_cores(prior_own).reshape(n_ep, cap, half), core
    ).reshape(rows, width)
    gg_prior, ug_prior = hidden_grads(prior_block, home_down[0], prior_act[0], prior_act[1])

    prior_entry = replica_expert[jnp.maximum(column - 1, 0)]
    keeps_own = replica_expert[column] == column
    takes_prior = (column > 0) & (prior_entry == column)

    def only(array, keep):
        return jnp.where(keep, array, jnp.zeros_like(array))

    all_x = jnp.concatenate([held[0], held[1], only(prior_x, takes_prior)])
    all_block = jnp.concatenate([block_home, block_spare, only(prior_block, takes_prior)])

    def stacked(a, b, c):
        return jnp.concatenate([a, only(b, keeps_own), only(c, takes_prior)])

    gate = lax.dot_general(
        all_x, stacked(gg_home, gg_spare, gg_prior), ROWS, preferred_element_type=F32
    )
    up = lax.dot_general(
        all_x, stacked(ug_home, ug_spare, ug_prior), ROWS, preferred_element_type=F32
    )
    down = lax.dot_general(
        stacked(home_act[2], spare_act[2], prior_act[2]), all_block, ROWS, preferred_element_type=F32
    )
    grad_gate_up = jnp.stack([gate, up])[None].astype(BF)
    return (input_grad, grad_gate_up, down[None].astype(BF))


def solution(mesh):
    placed = (
        P("ep", None),
        P("ep", None),
        P("ep", None),
        P(),
        P("ep", None, None, None, None),
        P("ep", None, None, "dp"),
        P("ep", "dp", None),
        P("ep", None, None, "dp"),
        P("ep", "dp", None),
    )
    return jax.shard_map(
        on_device,
        mesh=mesh,
        in_specs=placed,
        out_specs=(P("ep", None), P("ep", None, None, "dp"), P("ep", "dp", None)),
        check_vma=False,
    )
```

time: 440 us -> 214 us (0.49)
  waiting for transfers between devices: 315 us -> 26.8 us
  starting transfers between devices: 50.6 us -> 120 us
  between operations: 15.7 us -> 2.47 us
    psum x1 -> x0, waiting for transfers between devices: 276 us -> none  [on_device(): lax.psum(partial_rows.astype(jnp.float32).astype(jnp.bfloat16), 'dp')]
    ppermute x1 -> x10, starting transfers between devices: 13.2 us -> 73.8 us  [the longest x8 46.7 us: along_dp(): return lax.ppermute(array, 'dp', pairs)]
    all_to_all x2, waiting for transfers between devices: 39.1 us -> 13 us  [exchange(): return lax.all_to_all(array, 'ep', split_axis=0, concat_axis=0, tiled=True)]
    ppermute x1 -> x10, waiting for transfers between devices: 0.01 us -> 13.8 us  [the longest x2 9.95 us: to_next(): return lax.ppermute(array, 'ep', [(i, i + 1) for i in range(length - 1)])]
    all_to_all x2, starting transfers between devices: 37.4 us -> 46.2 us  [exchange(): return lax.all_to_all(array, 'ep', split_axis=0, concat_axis=0, tiled=True)]
    dot_general x18 -> x22, matrix products: 16.2 us -> 18.8 us  [the longest x3 3.66 us: hidden_grads(): hg = lax.dot_general(block, down, COLS, preferred_element_type=F32)]
  transfers between devices with their start and end apart: 4 -> 12, of which waited for: 3 -> 5; matrix products, arithmetic and copies ran while one was open for 7% -> 25% of each run, Pallas kernels for 0% -> 0%
where the time goes in v1:
time: 214 us; the launch traced here: 213 us
  starting transfers between devices  120 us (56%)
  local copies, waits for them, and re-layouts  31.6 us (15%)
  waiting for transfers between devices  26.8 us (13%)
  matrix products  18.8 us (9%)
  other arithmetic  13.3 us (6%)
  between operations  2.47 us (1%)
    ppermute x8, starting transfers between devices, along_dp(): return lax.ppermute(array, 'dp', pairs)  46.7 us
    all_to_all x2, starting transfers between devices, exchange(): return lax.all_to_all(array, 'ep', split_axis=0, concat_axis=0, tiled=True)  46.2 us
    ppermute x2, starting transfers between devices, to_next(): return lax.ppermute(array, 'ep', [(i, i + 1) for i in range(length - 1)])  27.1 us
    all_to_all x2, waiting for transfers between devices, exchange(): return lax.all_to_all(array, 'ep', split_axis=0, concat_axis=0, tiled=True)  13 us
    ppermute x2, waiting for transfers between devices, to_next(): return lax.ppermute(array, 'ep', [(i, i + 1) for i in range(length - 1)])  9.95 us
    another operation x4, local copies, waits for them, and re-layouts, back(): return jnp.stack([p.reshape(n_ep, cap, half) for p in parts], axis=1)  5.24 us
    unnamed x50, local copies, waits for them, and re-layouts  5.1 us
  transfers between devices with their start and end apart: 12, of which 5 were waited for; matrix products, arithmetic and copies ran while one was open for 25% of the time, Pallas kernels for 0%

profile of v1, /device:TPU:1, one launch (start us, length us, event | category | flops | bytes accessed | tf_op | source)
XLA Modules:
  0.0 213.0 jit_solution(17680701386388085061)
XLA Ops:
  5.2 24.0 %all-to-all-start = ((bf16[64,16,256]{2,1,0:T(8,128)(2,1)}), bf16[64,16,256]{2,1,0:T(8,128)(2,1)}, u32[]{:S(2)}, u32[]{:S(2)}) async-start(bf16[64,16,256]{2,1,0:T(8,128)(2,1)} %reshape.162), calls=%async_computation | async-start | bytes 1048576 | tf_op jit(solution)/shard_map/all_to_all | solution.py:27
  29.3 1.5 fusion.76
  31.0 10.0 %collective-permute-start.6 = (bf16[64,2,1024]{2,1,0:T(2,128)(2,1)S(1)}, bf16[64,2,1024]{2,1,0:T(2,128)(2,1)}, u32[]{:S(2)}, u32[]{:S(2)}) collective-permute-start(bf16[64,2,1024]{2,1,0:T(2,128)(2,1)S(1)} %dynamic-slice_bitcast_fusion.16), channel_id=1, source_target_pairs={{0,12},{12,24},{24,36},{36,48},{48,60},{60,72},{72,84},{84,96},{96... | collective-permute-start | bytes 786440 | tf_op jit(solution)/shard_map/ppermute | solution.py:23
  41.5 8.9 %collective-permute-done.6 = bf16[64,2,1024]{2,1,0:T(2,128)(2,1)} collective-permute-done((bf16[64,2,1024]{2,1,0:T(2,128)(2,1)S(1)}, bf16[64,2,1024]{2,1,0:T(2,128)(2,1)}, u32[]{:S(2)}, u32[]{:S(2)}) %collective-permute-start.6) | collective-permute-done | bytes 262176 | tf_op jit(solution)/shard_map/ppermute | solution.py:23
  50.4 10.1 %collective-permute-start.7 = (bf16[64,2,1024]{2,1,0:T(2,128)(2,1)}, bf16[64,2,1024]{2,1,0:T(2,128)(2,1)S(1)}, u32[]{:S(2)}, u32[]{:S(2)}) collective-permute-start(bf16[64,2,1024]{2,1,0:T(2,128)(2,1)} %collective-permute-done.6), channel_id=1, source_target_pairs={{0,1},{1,0},{2,3},{3,2},{4,5},{5,4},{6,7},{7,6},{8,9},{9,8},{10,11... | collective-permute-start | bytes 786440 | tf_op jit(solution)/shard_map/ppermute | solution.py:14
  63.3 2.0 squeeze.71
  65.4 1.9 fusion.19
  70.1 17.1 %collective-permute-start.8 = (bf16[64,8,256]{2,1,0:T(8,128)(2,1)S(1)}, bf16[64,8,256]{2,1,0:T(8,128)(2,1)}, u32[]{:S(2)}, u32[]{:S(2)}) collective-permute-start(bf16[64,8,256]{2,1,0:T(8,128)(2,1)S(1)} %slice_bitcast_fusion), channel_id=1, source_target_pairs={{0,12},{12,24},{24,36},{36,48},{48,60},{60,72},{72,84},{84,96},{96... | collective-permute-start | bytes 786440 | tf_op jit(solution)/shard_map/ppermute | solution.py:23
  87.2 2.2 %collective-permute-start = (bf16[64,16,256]{2,1,0:T(8,128)(2,1)}, bf16[64,16,256]{2,1,0:T(8,128)(2,1)S(1)}, u32[]{:S(2)}, u32[]{:S(2)}) collective-permute-start(bf16[64,16,256]{2,1,0:T(8,128)(2,1)} %all-to-all-done), channel_id=1, source_target_pairs={{0,1},{1,0},{2,3},{3,2},{4,5},{5,4},{6,7},{7,6},{8,9},{9,8},{10,11... | collective-permute-start | bytes 1572872 | tf_op jit(solution)/shard_map/ppermute | solution.py:14
  92.2 2.7 %collective-permute-start.9 = (bf16[64,8,256]{2,1,0:T(8,128)(2,1)}, bf16[64,8,256]{2,1,0:T(8,128)(2,1)}, u32[]{:S(2)}, u32[]{:S(2)}) collective-permute-start(bf16[64,8,256]{2,1,0:T(8,128)(2,1)} %collective-permute-done.8), channel_id=1, source_target_pairs={{0,1},{1,0},{2,3},{3,2},{4,5},{5,4},{6,7},{7,6},{8,9},{9,8},{10,11... | collective-permute-start | bytes 786440 | tf_op jit(solution)/shard_map/ppermute | solution.py:14
  94.9 1.9 broadcast_select_fusion.4
  96.8 2.0 select_n.142
  99.9 1.7 constant_dynamic-update-slice_fusion.1
  102.0 1.5 fusion.77
  103.5 2.1 reshape_squeeze.6
  106.6 2.0 broadcast_select_fusion.10
  110.8 2.1 convolution_add_fusion.2
  113.0 2.2 %stack_reshape.15 = f32[64,1,2,1024]{3,2,0,1:T(2,128)} reshape(f32[128,1024]{1,0:T(8,128)} %convolution_add_fusion.2) | data formatting | bytes 1048576 | tf_op jit(solution)/shard_map/stack;reshape | solution.py:109
  118.8 2.5 %pad_maximum_fusion.5 = bf16[64,2,2,1024]{3,2,1,0:T(2,128)(2,1)} fusion(bf16[64,1,2,1024]{3,2,1,0:T(2,128)(2,1)} %bitcast.114, bf16[64,1,2,1024]{3,2,1,0:T(2,128)(2,1)} %bitcast.115), kind=kLoop, calls=%fused_computation.23 | loop fusion | flops 262144 | bytes 1048576 | tf_op jit(solution)/shard_map/stack | solution.py:109
  121.3 2.0 convert_element_type.99
  123.4 2.1 collective-permute-start.1
  128.2 1.5 pad_maximum_fusion.1
  129.6 2.1 reshape.163
  131.7 2.0 add_convert_fusion
  133.7 22.2 %all-to-all-start.1 = ((bf16[64,16,256]{2,1,0:T(8,128)(2,1)}), bf16[64,16,256]{2,1,0:T(8,128)(2,1)}, u32[]{:S(2)}, u32[]{:S(2)}) async-start(bf16[64,16,256]{2,1,0:T(8,128)(2,1)} %add_convert_fusion), calls=%async_computation.1 | async-start | bytes 1048576 | tf_op jit(solution)/shard_map/all_to_all | solution.py:27
  159.8 1.4 fusion
  161.2 13.0 %all-to-all-done.1 = bf16[64,16,256]{2,1,0:T(8,128)(2,1)} async-done(((bf16[64,16,256]{2,1,0:T(8,128)(2,1)}), bf16[64,16,256]{2,1,0:T(8,128)(2,1)}, u32[]{:S(2)}, u32[]{:S(2)}) %all-to-all-start.1) | async-done | bytes 524320 | tf_op jit(solution)/shard_map/all_to_all | solution.py:27
  175.8 17.4 %collective-permute-start.2 = (bf16[16,1024]{1,0:T(8,128)(2,1)S(1)}, bf16[16,1024]{1,0:T(8,128)(2,1)S(1)}, u32[]{:S(2)}, u32[]{:S(2)}) collective-permute-start(bf16[16,1024]{1,0:T(8,128)(2,1)S(1)} %get-tuple-element.32), channel_id=1, source_target_pairs={{0,2},{1,3},{2,0},{3,1},{4,6},{5,7},{6,4},{7,5},{8,10},{9,11},{10,... | collective-permute-start | bytes 98312 | tf_op jit(solution)/shard_map/ppermute | solution.py:14
  194.5 2.1 collective-permute-start.4
  196.6 4.3 %collective-permute-start.3 = (bf16[16,1024]{1,0:T(8,128)(2,1)S(1)}, bf16[16,1024]{1,0:T(8,128)(2,1)S(1)}, u32[]{:S(2)}, u32[]{:S(2)}) collective-permute-start(bf16[16,1024]{1,0:T(8,128)(2,1)S(1)} %fusion.58), channel_id=1, source_target_pairs={{0,4},{1,5},{2,6},{3,7},{4,8},{5,9},{6,10},{7,11},{8,0},{9,1},{10,... | collective-permute-start | bytes 98312 | tf_op jit(solution)/shard_map/ppermute | solution.py:14
  201.9 3.2 %collective-permute-done.3 = bf16[16,1024]{1,0:T(8,128)(2,1)S(1)} collective-permute-done((bf16[16,1024]{1,0:T(8,128)(2,1)S(1)}, bf16[16,1024]{1,0:T(8,128)(2,1)S(1)}, u32[]{:S(2)}, u32[]{:S(2)}) %collective-permute-start.3) | collective-permute-done | bytes 32800 | tf_op jit(solution)/shard_map/ppermute | solution.py:14
  205.2 5.9 %collective-permute-start.5 = (bf16[16,1024]{1,0:T(8,128)(2,1)S(1)}, bf16[16,1024]{1,0:T(8,128)(2,1)S(1)}, u32[]{:S(2)}, u32[]{:S(2)}) collective-permute-start(bf16[16,1024]{1,0:T(8,128)(2,1)S(1)} %add_convert_fusion.1), channel_id=1, source_target_pairs={{0,1},{1,0},{2,3},{3,2},{4,5},{5,4},{6,7},{7,6},{8,9},{9,8},{10,11... | collective-permute-start | bytes 98312 | tf_op jit(solution)/shard_map/ppermute | solution.py:14
  (113 shorter events, 32.9 us)
Async XLA Ops:
  0.6 105.9 %copy-start = (bf16[1,128,2048]{2,1,0:T(8,128)(2,1)S(1)}, bf16[1,128,2048]{2,1,0:T(8,128)(2,1)}, u32[]{:S(2)}) copy-start(bf16[1,128,2048]{2,1,0:T(8,128)(2,1)} %param.17) | copy-start | bytes 1572868
  4.1 25.2 %copy-start.12 = (bf16[1,2,64,2,2048]{4,3,2,1,0:T(2,128)(2,1)S(1)}, bf16[1,2,64,2,2048]{4,3,2,1,0:T(2,128)(2,1)}, u32[]{:S(2)}) copy-start(bf16[1,2,64,2,2048]{4,3,2,1,0:T(2,128)(2,1)} %param.13) | copy-start | bytes 3145732
  5.2 63.8 %all-to-all-start = ((bf16[64,16,256]{2,1,0:T(8,128)(2,1)}), bf16[64,16,256]{2,1,0:T(8,128)(2,1)}, u32[]{:S(2)}, u32[]{:S(2)}) async-start(bf16[64,16,256]{2,1,0:T(8,128)(2,1)} %reshape.162), calls=%async_computation | async-start | bytes 1048576 | tf_op jit(solution)/shard_map/all_to_all | solution.py:27
  30.8 10.4 %copy-start.1 = (bf16[1,2,2048,128]{3,2,1,0:T(8,128)(2,1)S(1)}, bf16[1,2,2048,128]{3,2,1,0:T(8,128)(2,1)}, u32[]{:S(2)}) copy-start(bf16[1,2,2048,128]{3,2,1,0:T(8,128)(2,1)} %param.16) | copy-start | bytes 3145732
  31.0 19.4 %collective-permute-start.6 = (bf16[64,2,1024]{2,1,0:T(2,128)(2,1)S(1)}, bf16[64,2,1024]{2,1,0:T(2,128)(2,1)}, u32[]{:S(2)}, u32[]{:S(2)}) collective-permute-start(bf16[64,2,1024]{2,1,0:T(2,128)(2,1)S(1)} %dynamic-slice_bitcast_fusion.16), channel_id=1, source_target_pairs={{0,12},{12,24},{24,36},{36,48},{48,60},{60,72},{72,84},{84,96},{96... | collective-permute-start | bytes 786440 | tf_op jit(solution)/shard_map/ppermute | solution.py:23
  41.2 20.2 %copy-start.19 = (s32[64]{0:T(128)S(1)}, s32[64]{0:T(128)}, u32[]{:S(2)}) copy-start(s32[64]{0:T(128)} %param.12) | copy-start | bytes 772
  41.5 23.9 %copy-start.2 = (bf16[1,2,2048,128]{3,2,1,0:T(8,128)(2,1)S(1)}, bf16[1,2,2048,128]{3,2,1,0:T(8,128)(2,1)}, u32[]{:S(2)}) copy-start(bf16[1,2,2048,128]{3,2,1,0:T(8,128)(2,1)} %param.14) | copy-start | bytes 3145732
  50.4 16.9 %collective-permute-start.7 = (bf16[64,2,1024]{2,1,0:T(2,128)(2,1)}, bf16[64,2,1024]{2,1,0:T(2,128)(2,1)S(1)}, u32[]{:S(2)}, u32[]{:S(2)}) collective-permute-start(bf16[64,2,1024]{2,1,0:T(2,128)(2,1)} %collective-permute-done.6), channel_id=1, source_target_pairs={{0,1},{1,0},{2,3},{3,2},{4,5},{5,4},{6,7},{7,6},{8,9},{9,8},{10,11... | collective-permute-start | bytes 786440 | tf_op jit(solution)/shard_map/ppermute | solution.py:14
  69.0 21.2 %copy-start.3 = (bf16[1,2,2048,128]{3,2,1,0:T(8,128)(2,1)S(1)}, bf16[1,2,2048,128]{3,2,1,0:T(8,128)(2,1)}, u32[]{:S(2)}) copy-start(bf16[1,2,2048,128]{3,2,1,0:T(8,128)(2,1)} %param.14) | copy-start | bytes 3145732
  70.1 22.2 %collective-permute-start.8 = (bf16[64,8,256]{2,1,0:T(8,128)(2,1)S(1)}, bf16[64,8,256]{2,1,0:T(8,128)(2,1)}, u32[]{:S(2)}, u32[]{:S(2)}) collective-permute-start(bf16[64,8,256]{2,1,0:T(8,128)(2,1)S(1)} %slice_bitcast_fusion), channel_id=1, source_target_pairs={{0,12},{12,24},{24,36},{36,48},{48,60},{60,72},{72,84},{84,96},{96... | collective-permute-start | bytes 786440 | tf_op jit(solution)/shard_map/ppermute | solution.py:23
  87.2 7.7 %collective-permute-start = (bf16[64,16,256]{2,1,0:T(8,128)(2,1)}, bf16[64,16,256]{2,1,0:T(8,128)(2,1)S(1)}, u32[]{:S(2)}, u32[]{:S(2)}) collective-permute-start(bf16[64,16,256]{2,1,0:T(8,128)(2,1)} %all-to-all-done), channel_id=1, source_target_pairs={{0,1},{1,0},{2,3},{3,2},{4,5},{5,4},{6,7},{7,6},{8,9},{9,8},{10,11... | collective-permute-start | bytes 1572872 | tf_op jit(solution)/shard_map/ppermute | solution.py:14
  92.2 63.7 %collective-permute-start.9 = (bf16[64,8,256]{2,1,0:T(8,128)(2,1)}, bf16[64,8,256]{2,1,0:T(8,128)(2,1)}, u32[]{:S(2)}, u32[]{:S(2)}) collective-permute-start(bf16[64,8,256]{2,1,0:T(8,128)(2,1)} %collective-permute-done.8), channel_id=1, source_target_pairs={{0,1},{1,0},{2,3},{3,2},{4,5},{5,4},{6,7},{7,6},{8,9},{9,8},{10,11... | collective-permute-start | bytes 786440 | tf_op jit(solution)/shard_map/ppermute | solution.py:14
  99.9 1.7 copy-start.10
  103.5 3.1 %copy-start.16 = (f32[128,128]{1,0:T(8,128)S(1)}, f32[128,128]{1,0:T(8,128)}, u32[]{:S(2)}) copy-start(f32[128,128]{1,0:T(8,128)} %fusion.13) | copy-start | bytes 196612
  110.8 4.4 %copy-start.6 = (bf16[1,128,2048]{2,1,0:T(8,128)(2,1)S(1)}, bf16[1,128,2048]{2,1,0:T(8,128)(2,1)}, u32[]{:S(2)}) copy-start(bf16[1,128,2048]{2,1,0:T(8,128)(2,1)} %param.15) | copy-start | bytes 1572868
  113.0 3.6 %copy-start.4 = (bf16[1,2,2048,128]{3,2,1,0:T(8,128)(2,1)S(1)}, bf16[1,2,2048,128]{3,2,1,0:T(8,128)(2,1)}, u32[]{:S(2)}) copy-start(bf16[1,2,2048,128]{3,2,1,0:T(8,128)(2,1)} %param.14) | copy-start | bytes 3145732
  113.0 3.7 %copy-start.18 = (f32[128,128]{1,0:T(8,128)S(1)}, f32[128,128]{1,0:T(8,128)}, u32[]{:S(2)}) copy-start(f32[128,128]{1,0:T(8,128)} %fusion.19) | copy-start | bytes 196612
  115.2 1.4 copy-start.7
  123.4 8.4 %collective-permute-start.1 = (bf16[64,16,256]{2,1,0:T(8,128)(2,1)}, bf16[64,16,256]{2,1,0:T(8,128)(2,1)}, u32[]{:S(2)}, u32[]{:S(2)}) collective-permute-start(bf16[64,16,256]{2,1,0:T(8,128)(2,1)} %convert_element_type.99), channel_id=1, source_target_pairs={{0,1},{1,0},{2,3},{3,2},{4,5},{5,4},{6,7},{7,6},{8,9},{9,8},{10,11... | collective-permute-start | bytes 1572872 | tf_op jit(solution)/shard_map/ppermute | solution.py:14
  126.7 1.4 copy-start.11
  133.7 40.5 %all-to-all-start.1 = ((bf16[64,16,256]{2,1,0:T(8,128)(2,1)}), bf16[64,16,256]{2,1,0:T(8,128)(2,1)}, u32[]{:S(2)}, u32[]{:S(2)}) async-start(bf16[64,16,256]{2,1,0:T(8,128)(2,1)} %add_convert_fusion), calls=%async_computation.1 | async-start | bytes 1048576 | tf_op jit(solution)/shard_map/all_to_all | solution.py:27
  157.3 1.2 copy-start.5
  157.3 1.2 copy-start.17
  161.2 32.0 %copy-start.20 = (bf16[128,128]{1,0:T(8,128)(2,1)S(1)}, bf16[128,128]{1,0:T(8,128)(2,1)}, u32[]{:S(2)}) copy-start(bf16[128,128]{1,0:T(8,128)(2,1)} %get-tuple-element.21) | copy-start | bytes 98308
  175.8 18.7 %collective-permute-start.2 = (bf16[16,1024]{1,0:T(8,128)(2,1)S(1)}, bf16[16,1024]{1,0:T(8,128)(2,1)S(1)}, u32[]{:S(2)}, u32[]{:S(2)}) collective-permute-start(bf16[16,1024]{1,0:T(8,128)(2,1)S(1)} %get-tuple-element.32), channel_id=1, source_target_pairs={{0,2},{1,3},{2,0},{3,1},{4,6},{5,7},{6,4},{7,5},{8,10},{9,11},{10,... | collective-permute-start | bytes 98312 | tf_op jit(solution)/shard_map/ppermute | solution.py:14
  193.2 7.7 %copy-start.15 = (bf16[1,1,2048,128]{3,2,1,0:T(8,128)(2,1)S(1)}, bf16[1,1,2048,128]{3,2,1,0:T(8,128)(2,1)}, u32[]{:S(2)}) copy-start(bf16[1,1,2048,128]{3,2,1,0:T(8,128)(2,1)} %fusion) | copy-start | bytes 1572868
  194.5 16.6 %copy-start.9 = (bf16[128,2048]{1,0:T(8,128)(2,1)S(1)}, bf16[128,2048]{1,0:T(8,128)(2,1)}, u32[]{:S(2)}) copy-start(bf16[128,2048]{1,0:T(8,128)(2,1)} %reshape_squeeze.6) | copy-start | bytes 1572868
  194.5 16.6 %copy-start.13 = (bf16[128,2048]{1,0:T(8,128)(2,1)S(1)}, bf16[128,2048]{1,0:T(8,128)(2,1)}, u32[]{:S(2)}) copy-start(bf16[128,2048]{1,0:T(8,128)(2,1)} %reshape_squeeze.7) | copy-start | bytes 1572868
  194.5 16.6 %copy-start.22 = (bf16[128,128]{1,0:T(8,128)(2,1)S(1)}, bf16[128,128]{1,0:T(8,128)(2,1)}, u32[]{:S(2)}) copy-start(bf16[128,128]{1,0:T(8,128)(2,1)} %get-tuple-element.17) | copy-start | bytes 98308
  194.5 7.4 %collective-permute-start.4 = (bf16[16,1024]{1,0:T(8,128)(2,1)S(1)}, bf16[16,1024]{1,0:T(8,128)(2,1)S(1)}, u32[]{:S(2)}, u32[]{:S(2)}) collective-permute-start(bf16[16,1024]{1,0:T(8,128)(2,1)S(1)} %fusion.58), channel_id=1, source_target_pairs={{0,8},{1,9},{2,10},{3,11},{4,0},{5,1},{6,2},{7,3},{8,4},{9,5},{10,... | collective-permute-start | bytes 98312 | tf_op jit(solution)/shard_map/ppermute | solution.py:14
  196.6 8.6 %collective-permute-start.3 = (bf16[16,1024]{1,0:T(8,128)(2,1)S(1)}, bf16[16,1024]{1,0:T(8,128)(2,1)S(1)}, u32[]{:S(2)}, u32[]{:S(2)}) collective-permute-start(bf16[16,1024]{1,0:T(8,128)(2,1)S(1)} %fusion.58), channel_id=1, source_target_pairs={{0,4},{1,5},{2,6},{3,7},{4,8},{5,9},{6,10},{7,11},{8,0},{9,1},{10,... | collective-permute-start | bytes 98312 | tf_op jit(solution)/shard_map/ppermute | solution.py:14
  205.2 7.2 %collective-permute-start.5 = (bf16[16,1024]{1,0:T(8,128)(2,1)S(1)}, bf16[16,1024]{1,0:T(8,128)(2,1)S(1)}, u32[]{:S(2)}, u32[]{:S(2)}) collective-permute-start(bf16[16,1024]{1,0:T(8,128)(2,1)S(1)} %add_convert_fusion.1), channel_id=1, source_target_pairs={{0,1},{1,0},{2,3},{3,2},{4,5},{5,4},{6,7},{7,6},{8,9},{9,8},{10,11... | collective-permute-start | bytes 98312 | tf_op jit(solution)/shard_map/ppermute | solution.py:14
  (3 other events, 3.4 us)

commit v2 on v1

v2 whole, which is shorter than its diff:
```python
import jax
import jax.numpy as jnp
from jax import lax
from jax.experimental import pallas as pl
from jax.experimental.pallas import tpu as pltpu
from jax.sharding import PartitionSpec as P

BF = jnp.bfloat16
F32 = jnp.float32
NT = (((1,), (1,)), ((), ()))
TN = (((0,), (0,)), ((), ()))
GROUPS = 8
VMEM = pl.BlockSpec(memory_space=pltpu.VMEM)
ANY = pl.BlockSpec(memory_space=pl.ANY)
SMEM = pl.BlockSpec(memory_space=pltpu.SMEM)


def along_dp(array, to):
    pairs = [(2 * z + c, 2 * to(z)[0] + (c ^ to(z)[1])) for z in range(6) for c in range(2)]
    return lax.ppermute(array, "dp", pairs)


def swap_cores(array):
    return along_dp(array, lambda z: (z, 1))


def mirrored(e, dp):
    return 12 * e + (dp if e % 2 == 0 else 10 - dp + 2 * (dp % 2))


def to_next(array):
    length = lax.axis_size("ep")
    pairs = [
        (mirrored(e, dp), mirrored(e + 1, dp)) for e in range(length - 1) for dp in range(12)
    ]
    return lax.ppermute(array, ("ep", "dp"), pairs)


def exchange(array):
    length = lax.axis_size("ep")
    groups = [[mirrored(e, dp) for e in range(length)] for dp in range(12)]
    array = array.reshape(length, -1, 256)
    array = lax.all_to_all(
        array, ("ep", "dp"), split_axis=0, concat_axis=0, axis_index_groups=groups, tiled=True
    )
    return array.reshape(-1, 256)


def dot(a, b, dims=(((1,), (0,)), ((), ()))):
    return lax.dot_general(a, b, dims, preferred_element_type=F32)


def half_at(core):
    return pl.ds(pl.multiple_of(core * 1024, 1024), 1024)


def by_slot():
    row = lax.broadcasted_iota(jnp.int32, (128, 128), 0)
    col = lax.broadcasted_iota(jnp.int32, (128, 128), 1)
    return (col == 16 * (row % 8) + 2 * (row // 16) + row // 8 % 2).astype(F32).astype(BF)


def by_source(kinds):
    row = lax.broadcasted_iota(jnp.int32, (64 * kinds, 64 * kinds), 0)
    col = lax.broadcasted_iota(jnp.int32, (64 * kinds, 64 * kinds), 1)
    want = 8 * kinds * (row // 2 % 8) + 8 * (row // 64) + 4 * (row % 2) + row // 16 % 4
    return (col == want).astype(F32).astype(BF)


def by_prior():
    row = lax.broadcasted_iota(jnp.int32, (128, 128), 0)
    col = lax.broadcasted_iota(jnp.int32, (128, 128), 1)
    return (col == 16 * (row % 8) + row // 8).astype(F32).astype(BF)


def slots():
    return lax.broadcasted_iota(jnp.int32, (128, 16), 0)


def places_of(slot, routes):
    named = jnp.zeros(slot.shape, F32)
    for k in range(8):
        named = named + jnp.where(slot == routes[k : k + 1, :], 1.0, 0.0)
    before = lax.broadcasted_iota(jnp.int32, (16, 16), 0) < lax.broadcasted_iota(
        jnp.int32, (16, 16), 1
    )
    earlier = dot(named.astype(BF), before.astype(F32).astype(BF))
    return [jnp.where(earlier == p, named, 0.0) for p in range(2)]


def routed(slot, routes, probs, half):
    prob = jnp.zeros(slot.shape, F32)
    for k in range(8):
        prob = prob + jnp.where(slot == routes[k : k + 1, :], probs[k : k + 1, :], 0.0)
    places = places_of(slot, routes)
    rows = []
    for place in places:
        row_prob = jnp.sum(place * prob, axis=1, keepdims=True)
        rows.append((dot(place.astype(BF), half) * row_prob).astype(BF))
    return places, rows


def blocks_of(rows, g):
    parts = [
        rows[p][16 * g : 16 * g + 16, 256 * f : 256 * f + 256] for p in range(2) for f in range(4)
    ]
    return jnp.concatenate(parts)


def prep_kernel(routes, probs, out_grad, outgoing):
    half = out_grad[:, half_at(lax.axis_index("dp") % 2)]
    table = by_slot()
    _, rows = routed(slots(), routes, probs, half)
    prior = 2 * lax.broadcasted_iota(jnp.int32, (64, 16), 0) - 1
    _, prior_rows = routed(prior, routes, probs, half)
    prior_table = by_prior()
    for g in range(4):
        held = [dot(table, blocks_of(rows, 2 * g + h)).astype(BF) for h in range(2)]
        extra = dot(prior_table, blocks_of(prior_rows, g)).astype(BF)
        for h in range(2):
            for c in range(8):
                at = 24 * (16 * g + 8 * h + c)
                outgoing[at : at + 16, :] = held[h][16 * c : 16 * c + 16, :]
                outgoing[at + 16 : at + 24, :] = extra[64 * h + 8 * c : 64 * h + 8 * c + 8, :]


def act(x, w_gate, w_up):
    gate = dot(x, w_gate)
    up = dot(x, w_up)
    sig = jax.nn.sigmoid(gate)
    active = gate * sig
    slope = up * sig * (1.0 + gate * (1.0 - sig))
    return active, slope, (active * up).astype(BF)


def act_kernel(x, home_gu, spare_gu, routes, active, slope, hidden, place_out):
    for p, place in enumerate(places_of(slots(), routes)):
        place_out[128 * p : 128 * p + 128, :] = place.astype(BF)
    for j, w in enumerate((home_gu, spare_gu)):
        a, s, h = act(x[128 * j : 128 * j + 128, :], w[0], w[1])
        active[128 * j : 128 * j + 128, :] = a
        slope[128 * j : 128 * j + 128, :] = s
        hidden[128 * j : 128 * j + 128, :] = h


def rows_kernel(
    own_in,
    other_in,
    active_in,
    slope_in,
    home_d,
    spare_d,
    home_gu,
    spare_gu,
    sent_out,
    kept_out,
    grads_out,
    block_out,
    got,
    active,
    slope,
    w_d,
    w_gu,
    block,
    sent,
    kept,
    grads,
    sems,
    out_sems,
):
    core = lax.axis_index("dp") % 2
    here, there = half_at(core), half_at(1 - core)
    pairs = [
        (own_in, got.at[0]),
        (other_in, got.at[1]),
        (home_d, w_d.at[0]),
        (slope_in, slope),
        (active_in, active),
        (home_gu, w_gu.at[0]),
        (spare_d, w_d.at[1]),
        (spare_gu, w_gu.at[1]),
    ]
    loads = [pltpu.make_async_copy(a, b, sems.at[i]) for i, (a, b) in enumerate(pairs)]
    for load in loads:
        load.start()
    table = by_source(3)
    for i, at in enumerate((here, there)):
        loads[i].wait()
        for g in range(GROUPS):
            rows = dot(table, got[i, 192 * g : 192 * g + 192, :]).astype(BF)
            for j in range(3):
                parts = [rows[64 * j + 16 * f : 64 * j + 16 * f + 16, :] for f in range(4)]
                block[128 * j + 16 * g : 128 * j + 16 * g + 16, at] = jnp.concatenate(parts, axis=1)
    stores = [pltpu.make_async_copy(block, block_out, out_sems.at[0])]
    stores[0].start()
    for j in range(2):
        mine = pl.ds(128 * j, 128)
        for i in ((2, 3, 4) if j == 0 else (6,)):
            loads[i].wait()
        hidden_grad = dot(block[mine, :], w_d[j], NT)
        both = jnp.concatenate(
            [(hidden_grad * slope[mine, :]).astype(BF), (hidden_grad * active[mine, :]).astype(BF)],
            axis=1,
        )
        grads[mine, :] = both
        loads[5 if j == 0 else 7].wait()
        weights = jnp.concatenate([w_gu[j, 0, here, :], w_gu[j, 1, here, :]], axis=1)
        kept[mine, :] = dot(both, weights, NT)
        weights = jnp.concatenate([w_gu[j, 0, there, :], w_gu[j, 1, there, :]], axis=1)
        sent[mine, :] = dot(both, weights, NT).astype(BF)
        for i, (a, b) in enumerate(((kept, kept_out), (sent, sent_out), (grads, grads_out))):
            store = pltpu.make_async_copy(a.at[mine], b.at[mine], out_sems.at[1 + 3 * j + i])
            store.start()
            stores.append(store)
    for store in stores:
        store.wait()


def pair_kernel(kept, got, outgoing):
    table = by_source(2)
    for g in range(GROUPS):
        parts = []
        for j in range(2):
            at = slice(128 * j + 16 * g, 128 * j + 16 * g + 16)
            total = (kept[at, :] + got[at, :].astype(F32)).astype(BF)
            parts += [total[:, 256 * f : 256 * f + 256] for f in range(4)]
        outgoing[128 * g : 128 * g + 128, :] = dot(table, jnp.concatenate(parts), TN).astype(BF)


def combine_kernel(returned, place, mine, low, rows):
    table = by_slot()
    for g in range(GROUPS):
        back = dot(table, returned[128 * g : 128 * g + 128, :], TN).astype(BF)
        for p in range(2):
            rows[128 * p + 16 * g : 128 * p + 16 * g + 16, :] = jnp.concatenate(
                [back[16 * (4 * p + f) : 16 * (4 * p + f) + 16, :] for f in range(4)], axis=1
            )
    total = dot(place[...], rows[...], TN)
    mine[...] = total
    low[...] = total.astype(BF)


def weights_kernel(
    experts,
    x,
    x_own,
    x_other,
    block,
    grads,
    hidden,
    home_gu,
    home_d,
    grad_gu,
    grad_d,
    x_prior,
):
    core = lax.axis_index("dp") % 2
    x_prior[pl.ds(pl.multiple_of(64 * core, 64), 64), :] = x_own[...]
    x_prior[pl.ds(pl.multiple_of(64 - 64 * core, 64), 64), :] = x_other[...]
    column = lax.axis_index("ep")
    keeps_own = experts[column] == column
    takes_prior = (column > 0) & (experts[jnp.maximum(column - 1, 0)] == column)
    active, slope, hidden_prior = act(x_prior[...], home_gu[0], home_gu[1])
    hidden_grad = dot(block[256:384, :], home_d[...], NT)
    grads_prior = jnp.concatenate(
        [(hidden_grad * slope).astype(BF), (hidden_grad * active).astype(BF)], axis=1
    )

    def only(keep, array):
        return jnp.where(keep, array, jnp.zeros_like(array))

    grads_spare = only(keeps_own, grads[128:256, :])
    grads_prior = only(takes_prior, grads_prior)
    hidden_spare = only(keeps_own, hidden[128:256, :])
    hidden_prior = only(takes_prior, hidden_prior)
    all_grads = jnp.concatenate([grads[0:128, :], grads_spare, grads_prior])
    all_hidden = jnp.concatenate([hidden[0:128, :], hidden_spare, hidden_prior])
    for i in range(8):
        at = slice(256 * i, 256 * i + 256)
        rows = jnp.concatenate([x[:, at], x_prior[:, at]])
        total = dot(rows, all_grads, TN).astype(BF)
        grad_gu[0, at, :] = total[:, :128]
        grad_gu[1, at, :] = total[:, 128:]
        grad_d[:, at] = dot(all_hidden, block[:, at], TN).astype(BF)


def finish_kernel(own, other, result):
    core = lax.axis_index("dp") % 2
    result[:, half_at(core)] = own[...]
    result[:, half_at(1 - core)] = other[...]


def shape(dims, kind=BF):
    return jax.ShapeDtypeStruct(dims, kind)


def call(kernel, outs, flops, nbytes, specs, scratch=(), into=None, vmem=60):
    return pl.pallas_call(
        kernel,
        out_shape=outs,
        in_specs=specs,
        out_specs=jax.tree.map(lambda _: VMEM, outs) if into is None else into,
        scratch_shapes=scratch,
        cost_estimate=pl.CostEstimate(flops=flops, bytes_accessed=nbytes, transcendentals=0),
        compiler_params=pltpu.CompilerParams(vmem_limit_bytes=vmem << 20),
    )


def on_device(
    out_grad,
    route_probs,
    routes,
    replica_expert,
    saved_inputs,
    home_gate_up,
    home_down,
    replica_gate_up,
    replica_down,
):
    home_gu, home_d = home_gate_up[0], home_down[0]
    spare_gu, spare_d = replica_gate_up[0], replica_down[0]

    core = lax.axis_index("dp") % 2
    x_part = lax.dynamic_slice_in_dim(saved_inputs[0, 1], core * 32, 32, 0)
    x_part, routes, route_probs = lax.optimization_barrier((x_part, routes, route_probs))
    x_part = to_next(x_part)

    outgoing = call(prep_kernel, shape((1536, 256)), 10**6, 10**6, [VMEM] * 3)(
        routes.T, route_probs.T, out_grad
    )
    incoming = exchange(outgoing)

    saved, _ = lax.optimization_barrier((saved_inputs, outgoing))
    x = saved.reshape(256, 2048)
    active, slope, hidden, place = call(
        act_kernel,
        (
            shape((256, 128), F32),
            shape((256, 128), F32),
            shape((256, 128)),
            shape((256, 16)),
        ),
        10**11,
        4 * 10**6,
        [VMEM] * 4,
    )(x, home_gu, spare_gu, routes.T)
    incoming, active, x_part = lax.optimization_barrier((incoming, active, x_part))

    other = swap_cores(incoming)
    sent, kept, grads, block = call(
        rows_kernel,
        (
            shape((256, 1024)),
            shape((256, 1024), F32),
            shape((256, 256)),
            shape((384, 2048)),
        ),
        10**9,
        8 * 10**6,
        [ANY] * 8,
        [
            pltpu.VMEM((2, 1536, 256), BF),
            pltpu.VMEM((256, 128), F32),
            pltpu.VMEM((256, 128), F32),
            pltpu.VMEM((2, 128, 2048), BF),
            pltpu.VMEM((2, 2, 2048, 128), BF),
            pltpu.VMEM((384, 2048), BF),
            pltpu.VMEM((256, 1024), BF),
            pltpu.VMEM((256, 1024), F32),
            pltpu.VMEM((256, 256), BF),
            pltpu.SemaphoreType.DMA((8,)),
            pltpu.SemaphoreType.DMA((7,)),
        ],
        (ANY, ANY, ANY, ANY),
    )(incoming, other, active, slope, home_d, spare_d, home_gu, spare_gu)
    got = swap_cores(sent)
    pair = call(pair_kernel, shape((1024, 256)), 10**8, 2 * 10**6, [VMEM] * 2, vmem=28)(kept, got)
    returned = exchange(pair)

    x_part, _ = lax.optimization_barrier((x_part, pair))
    grad_gu, grad_d = call(
        weights_kernel,
        (shape((2, 2048, 128)), shape((128, 2048))),
        10**8,
        10**6,
        [SMEM] + [VMEM] * 8,
        [pltpu.VMEM((128, 2048), BF)],
    )(
        replica_expert,
        x,
        x_part.reshape(64, 2048),
        swap_cores(x_part).reshape(64, 2048),
        block,
        grads,
        hidden,
        home_gu,
        home_d,
    )
    returned, grad_gu = lax.optimization_barrier((returned, grad_gu))

    mine, low = call(
        combine_kernel,
        (shape((16, 1024), F32), shape((16, 1024))),
        10**8,
        10**6,
        [VMEM] * 2,
        [pltpu.VMEM((256, 1024), BF)],
        vmem=28,
    )(returned, place)
    total = mine + along_dp(low, lambda z: (z ^ 1, 0)).astype(F32)
    low = total.astype(BF)
    one = along_dp(low, lambda z: ((z + 2) % 6, 0))
    two = along_dp(low, lambda z: ((z + 4) % 6, 0))
    total = (total + one.astype(F32) + two.astype(F32)).astype(BF)
    input_grad = call(finish_kernel, shape((16, 2048)), 10**3, 10**5, [VMEM] * 2, vmem=28)(
        total, swap_cores(total)
    )
    return (input_grad, grad_gu[None], grad_d[None])


def solution(mesh):
    placed = (
        P("ep", None),
        P("ep", None),
        P("ep", None),
        P(),
        P("ep", None, None, None, None),
        P("ep", None, None, "dp"),
        P("ep", "dp", None),
        P("ep", None, None, "dp"),
        P("ep", "dp", None),
    )
    return jax.shard_map(
        on_device,
        mesh=mesh,
        in_specs=placed,
        out_specs=(P("ep", None), P("ep", None, None, "dp"), P("ep", "dp", None)),
        check_vma=False,
    )
```

time: 214 us -> 130 us (0.61)
  starting transfers between devices: 120 us -> 53.1 us
  local copies, waits for them, and re-layouts: 31.6 us -> 6.53 us
  waiting for transfers between devices: 26.8 us -> 51.2 us
  matrix products: 18.8 us -> 0 us
  Pallas kernels: 0 us -> 18.1 us
  other arithmetic: 13.3 us -> 0.03 us
    all_to_all x2, starting transfers between devices: 46.2 us -> 17.4 us  [exchange(): lax.all_to_all(array, ('ep', 'dp'), split_axis=0, concat_axis=0, axis_ind...]
    ppermute x8 -> x7, starting transfers between devices: 46.7 us -> 20.5 us  [along_dp(): return lax.ppermute(array, 'dp', pairs)]
    dot_general x22 -> x0, matrix products: 18.8 us -> none  [the longest x3 3.66 us: hidden_grads(): hg = lax.dot_general(block, down, COLS, preferred_element_type=F32)]
    pallas_call x0 -> x7, Pallas kernels: none -> 18.1 us  [the longest x1 5.16 us: on_device(): call(weights_kernel, (shape((2, 2048, 128)), shape((128, 2048))), 10 ** 8...]
    ppermute x2 -> x1, starting transfers between devices: 27.1 us -> 15.3 us  [to_next(): return lax.ppermute(array, ('ep', 'dp'), pairs)]
    all_to_all x2, waiting for transfers between devices: 13 us -> 23.4 us  [exchange(): lax.all_to_all(array, ('ep', 'dp'), split_axis=0, concat_axis=0, axis_ind...]
    another operation x6 -> x0, local copies, waits for them, and re-layouts: 8.31 us -> none  [the longest x4 5.24 us: back(): return jnp.stack([p.reshape(n_ep, cap, half) for p in parts], axis=1)]
    ppermute x8 -> x7, waiting for transfers between devices: 3.89 us -> 12.2 us  [along_dp(): return lax.ppermute(array, 'dp', pairs)]
  transfers between devices with their start and end apart: 12 -> 10, of which waited for: 5 -> 9; matrix products, arithmetic and copies ran while one was open for 25% -> 2% of each run, Pallas kernels for 0% -> 9%
where the time goes in v2:
time: 130 us
  starting transfers between devices  53.1 us (41%)
  waiting for transfers between devices  51.2 us (39%)
  Pallas kernels  18.1 us (14%)
  local copies, waits for them, and re-layouts  6.53 us (5%)
    all_to_all x2, waiting for transfers between devices, exchange(): lax.all_to_all(array, ('ep', 'dp'), split_axis=0, concat_axis=0, axis_ind...  23.4 us
    ppermute x7, starting transfers between devices, along_dp(): return lax.ppermute(array, 'dp', pairs)  20.5 us
    all_to_all x2, starting transfers between devices, exchange(): lax.all_to_all(array, ('ep', 'dp'), split_axis=0, concat_axis=0, axis_ind...  17.4 us
    ppermute x1, waiting for transfers between devices, to_next(): return lax.ppermute(array, ('ep', 'dp'), pairs)  15.7 us
    ppermute x1, starting transfers between devices, to_next(): return lax.ppermute(array, ('ep', 'dp'), pairs)  15.3 us
    ppermute x7, waiting for transfers between devices, along_dp(): return lax.ppermute(array, 'dp', pairs)  12.2 us
    pallas_call x1, Pallas kernels, on_device(): call(weights_kernel, (shape((2, 2048, 128)), shape((128, 2048))), 10 ** 8...  5.16 us
    pallas_call x1, Pallas kernels, on_device(): call(rows_kernel, (shape((256, 1024)), shape((256, 1024), F32), shape((25...  4.71 us
  transfers between devices with their start and end apart: 10, of which 9 were waited for; matrix products, arithmetic and copies ran while one was open for 2% of the time, Pallas kernels for 9%

profile of v2, /device:TPU:1, one launch (start us, length us, event | category | flops | bytes accessed | tf_op | source)
XLA Modules:
  0.0 129.8 jit_solution(631051558856957119)
XLA Ops:
  0.7 1.4 %slice.3 = bf16[1,1,64,2,2048]{4,3,2,1,0:T(2,128)(2,1)S(1)} slice(bf16[1,2,64,2,2048]{4,3,2,1,0:T(2,128)(2,1)} %param.13), slice={[0:1], [1:2], [0:64], [0:2], [0:2048]} | slice | bytes 1048576 | tf_op jit(solution)/shard_map/slice | solution.py:324
  2.3 15.3 %collective-permute-start = (bf16[32,2,2048]{2,1,0:T(2,128)(2,1)S(1)}, bf16[32,2,2048]{2,1,0:T(2,128)(2,1)S(1)}, u32[]{:S(2)}, u32[]{:S(2)}) collective-permute-start(bf16[32,2,2048]{2,1,0:T(2,128)(2,1)S(1)} %dynamic-slice_bitcast_fusion), channel_id=1, source_target_pairs={{0,22},{1,23},{2,20},{3,21},{4,18},{5,19},{6,16},{7,17},{8,14},{9,... | collective-permute-start | bytes 786440 | tf_op jit(solution)/shard_map/ppermute | solution.py:36
  17.6 2.7 %shard_map.112 = bf16[1536,256]{1,0:T(8,128)(2,1)} custom-call(s32[8,16]{1,0:T(8,128)} %bitcast.27, f32[8,16]{1,0:T(8,128)} %bitcast.26, bf16[16,2048]{1,0:T(8,128)(2,1)} %out_grad.1), custom_call_target="tpu_custom_call" | custom-call | flops 1000000 | bytes 1000000 | tf_op jit(solution)/shard_map/pallas_call | solution.py:328
  20.3 10.3 %all-to-all-start = ((bf16[64,24,256]{2,1,0:T(8,128)(2,1)}), bf16[64,24,256]{2,1,0:T(8,128)(2,1)S(1)}, u32[]{:S(2)}, u32[]{:S(2)}) async-start(bf16[64,24,256]{2,1,0:T(8,128)(2,1)} %bitcast.20), calls=%async_computation | async-start | bytes 1572864 | tf_op jit(solution)/shard_map/all_to_all | solution.py:43
  30.6 1.2 reshape.30.x
  31.8 3.3 %shard_map.113 = (f32[256,128]{1,0:T(8,128)}, f32[256,128]{1,0:T(8,128)}, bf16[256,128]{1,0:T(8,128)(2,1)}, bf16[256,16]{1,0:T(8,128)(2,1)}) custom-call(bf16[256,2048]{1,0:T(8,128)(2,1)} %reshape.30.x, bf16[2,2048,128]{2,1,0:T(8,128)(2,1)} %bitcast.15, bf16[2,2048,128]{2,1,0:T(8,128)(2,1)} %bitcast.23, s32[8,16]{1,0:T(8,128)} %bitcast.28), custom_call_target="tpu_custom_call" | custom-call | flops 99999997952 | bytes 4000000 | tf_op jit(solution)/shard_map/pallas_call | solution.py:335
  35.1 15.7 %collective-permute-done = bf16[32,2,2048]{2,1,0:T(2,128)(2,1)S(1)} collective-permute-done((bf16[32,2,2048]{2,1,0:T(2,128)(2,1)S(1)}, bf16[32,2,2048]{2,1,0:T(2,128)(2,1)S(1)}, u32[]{:S(2)}, u32[]{:S(2)}) %collective-permute-start) | collective-permute-done | bytes 262176 | tf_op jit(solution)/shard_map/ppermute | solution.py:36
  50.7 16.4 %all-to-all-done = bf16[64,24,256]{2,1,0:T(8,128)(2,1)S(1)} async-done(((bf16[64,24,256]{2,1,0:T(8,128)(2,1)}), bf16[64,24,256]{2,1,0:T(8,128)(2,1)S(1)}, u32[]{:S(2)}, u32[]{:S(2)}) %all-to-all-start) | async-done | bytes 786464 | tf_op jit(solution)/shard_map/all_to_all | solution.py:43
  67.1 2.7 %collective-permute-start.1 = (bf16[1536,256]{1,0:T(8,128)(2,1)S(1)}, bf16[1536,256]{1,0:T(8,128)(2,1)S(1)}, u32[]{:S(2)}, u32[]{:S(2)}) collective-permute-start(bf16[1536,256]{1,0:T(8,128)(2,1)S(1)} %bitcast.18), channel_id=1, source_target_pairs={{0,1},{1,0},{2,3},{3,2},{4,5},{5,4},{6,7},{7,6},{8,9},{9,8},{10,11... | collective-permute-start | bytes 2359304 | tf_op jit(solution)/shard_map/ppermute | solution.py:20
  69.8 1.9 %collective-permute-done.1.other_in = bf16[1536,256]{1,0:T(8,128)(2,1)S(1)} collective-permute-done((bf16[1536,256]{1,0:T(8,128)(2,1)S(1)}, bf16[1536,256]{1,0:T(8,128)(2,1)S(1)}, u32[]{:S(2)}, u32[]{:S(2)}) %collective-permute-start.1) | collective-permute-done | bytes 786464 | tf_op jit(solution)/shard_map/ppermute | solution.py:20
  71.7 0.9 copy-done.4
  72.6 4.7 %shard_map.114 = (bf16[256,1024]{1,0:T(8,128)(2,1)}, f32[256,1024]{1,0:T(8,128)}, bf16[256,256]{1,0:T(8,128)(2,1)}, bf16[384,2048]{1,0:T(8,128)(2,1)}) custom-call(bf16[1536,256]{1,0:T(8,128)(2,1)} %bitcast.19, bf16[1536,256]{1,0:T(8,128)(2,1)} %copy-done.4, f32[256,128]{1,0:T(8,128)} %get-tuple-element.31.active_in, f32[256,128]{1,0:T(8,128)} %get-tuple-element.32.slope_in, ...), custom_call_target="tpu_custom_call" | custom-call | flops 1000000000 | bytes 8000000 | tf_op jit(solution)/shard_map/pallas_call | solution.py:350
  77.3 2.3 %collective-permute-start.2 = (bf16[256,1024]{1,0:T(8,128)(2,1)}, bf16[256,1024]{1,0:T(8,128)(2,1)S(1)}, u32[]{:S(2)}, u32[]{:S(2)}) collective-permute-start(bf16[256,1024]{1,0:T(8,128)(2,1)} %get-tuple-element.34), channel_id=1, source_target_pairs={{0,1},{1,0},{2,3},{3,2},{4,5},{5,4},{6,7},{7,6},{8,9},{9,8},{10,11... | collective-permute-start | bytes 1572872 | tf_op jit(solution)/shard_map/ppermute | solution.py:20
  79.6 1.7 %collective-permute-done.2.got = bf16[256,1024]{1,0:T(8,128)(2,1)S(1)} collective-permute-done((bf16[256,1024]{1,0:T(8,128)(2,1)}, bf16[256,1024]{1,0:T(8,128)(2,1)S(1)}, u32[]{:S(2)}, u32[]{:S(2)}) %collective-permute-start.2) | collective-permute-done | bytes 524320 | tf_op jit(solution)/shard_map/ppermute | solution.py:20
  81.3 1.2 copy-done
  82.5 1.1 shard_map.115
  83.7 7.1 %all-to-all-start.1 = ((bf16[64,16,256]{2,1,0:T(8,128)(2,1)}), bf16[64,16,256]{2,1,0:T(8,128)(2,1)S(1)}, u32[]{:S(2)}, u32[]{:S(2)}) async-start(bf16[64,16,256]{2,1,0:T(8,128)(2,1)} %bitcast.9), calls=%async_computation.1 | async-start | bytes 1048576 | tf_op jit(solution)/shard_map/all_to_all | solution.py:43
  90.8 2.6 %collective-permute-start.3 = (bf16[32,2,2048]{2,1,0:T(2,128)(2,1)S(1)}, bf16[32,2,2048]{2,1,0:T(2,128)(2,1)S(1)}, u32[]{:S(2)}, u32[]{:S(2)}) collective-permute-start(bf16[32,2,2048]{2,1,0:T(2,128)(2,1)S(1)} %collective-permute-done), channel_id=1, source_target_pairs={{0,1},{1,0},{2,3},{3,2},{4,5},{5,4},{6,7},{7,6},{8,9},{9,8},{10,11... | collective-permute-start | bytes 786440 | tf_op jit(solution)/shard_map/ppermute | solution.py:20
  93.4 0.8 reshape.33.x_own
  94.2 0.3 collective-permute-done.3
  94.5 0.8 reshape.34.x_other
  95.3 5.2 %shard_map.116 = (bf16[2,2048,128]{2,1,0:T(8,128)(2,1)}, bf16[128,2048]{1,0:T(8,128)(2,1)}) custom-call(s32[64]{0:T(128)} %experts.1, bf16[256,2048]{1,0:T(8,128)(2,1)} %reshape.30.x, bf16[64,2048]{1,0:T(8,128)(2,1)} %reshape.33.x_own, bf16[64,2048]{1,0:T(8,128)(2,1)} %reshape.34.x_other, bf16[384,2048]{1,0:T(8,128)(2,1)} %get-tuple-element.37.block, ...), custom_call_target="tpu_custom_call" | custom-call | flops 100000000 | bytes 1000000 | tf_op jit(solution)/shard_map/pallas_call | solution.py:381
  100.5 7.0 %all-to-all-done.1 = bf16[64,16,256]{2,1,0:T(8,128)(2,1)S(1)} async-done(((bf16[64,16,256]{2,1,0:T(8,128)(2,1)}), bf16[64,16,256]{2,1,0:T(8,128)(2,1)S(1)}, u32[]{:S(2)}, u32[]{:S(2)}) %all-to-all-start.1) | async-done | bytes 524320 | tf_op jit(solution)/shard_map/all_to_all | solution.py:43
  107.5 0.5 shard_map.117
  108.0 1.9 %collective-permute-start.4 = (bf16[16,1024]{1,0:T(8,128)(2,1)S(1)}, bf16[16,1024]{1,0:T(8,128)(2,1)S(1)}, u32[]{:S(2)}, u32[]{:S(2)}) collective-permute-start(bf16[16,1024]{1,0:T(8,128)(2,1)S(1)} %get-tuple-element.44), channel_id=1, source_target_pairs={{0,2},{1,3},{2,0},{3,1},{4,6},{5,7},{6,4},{7,5},{8,10},{9,11},{10,... | collective-permute-start | bytes 98312 | tf_op jit(solution)/shard_map/ppermute | solution.py:20
  109.9 2.7 %collective-permute-done.4 = bf16[16,1024]{1,0:T(8,128)(2,1)S(1)} collective-permute-done((bf16[16,1024]{1,0:T(8,128)(2,1)S(1)}, bf16[16,1024]{1,0:T(8,128)(2,1)S(1)}, u32[]{:S(2)}, u32[]{:S(2)}) %collective-permute-start.4) | collective-permute-done | bytes 32800 | tf_op jit(solution)/shard_map/ppermute | solution.py:20
  112.7 1.9 %collective-permute-start.6 = (bf16[16,1024]{1,0:T(8,128)(2,1)S(1)}, bf16[16,1024]{1,0:T(8,128)(2,1)S(1)}, u32[]{:S(2)}, u32[]{:S(2)}) collective-permute-start(bf16[16,1024]{1,0:T(8,128)(2,1)S(1)} %fusion), channel_id=1, source_target_pairs={{0,8},{1,9},{2,10},{3,11},{4,0},{5,1},{6,2},{7,3},{8,4},{9,5},{10,... | collective-permute-start | bytes 98312 | tf_op jit(solution)/shard_map/ppermute | solution.py:20
  114.6 4.3 %collective-permute-start.5 = (bf16[16,1024]{1,0:T(8,128)(2,1)S(1)}, bf16[16,1024]{1,0:T(8,128)(2,1)S(1)}, u32[]{:S(2)}, u32[]{:S(2)}) collective-permute-start(bf16[16,1024]{1,0:T(8,128)(2,1)S(1)} %fusion), channel_id=1, source_target_pairs={{0,4},{1,5},{2,6},{3,7},{4,8},{5,9},{6,10},{7,11},{8,0},{9,1},{10,... | collective-permute-start | bytes 98312 | tf_op jit(solution)/shard_map/ppermute | solution.py:20
  118.9 4.6 %collective-permute-done.5 = bf16[16,1024]{1,0:T(8,128)(2,1)S(1)} collective-permute-done((bf16[16,1024]{1,0:T(8,128)(2,1)S(1)}, bf16[16,1024]{1,0:T(8,128)(2,1)S(1)}, u32[]{:S(2)}, u32[]{:S(2)}) %collective-permute-start.5) | collective-permute-done | bytes 32800 | tf_op jit(solution)/shard_map/ppermute | solution.py:20
  123.5 4.8 %collective-permute-start.7 = (bf16[16,1024]{1,0:T(8,128)(2,1)S(1)}, bf16[16,1024]{1,0:T(8,128)(2,1)S(1)}, u32[]{:S(2)}, u32[]{:S(2)}) collective-permute-start(bf16[16,1024]{1,0:T(8,128)(2,1)S(1)} %add_convert_fusion.own), channel_id=1, source_target_pairs={{0,1},{1,0},{2,3},{3,2},{4,5},{5,4},{6,7},{7,6},{8,9},{9,8},{10,11... | collective-permute-start | bytes 98312 | tf_op jit(solution)/shard_map/ppermute | solution.py:20
  128.4 0.8 collective-permute-done.7.other
  129.2 0.6 shard_map.118
  (12 shorter events, 0.2 us)
Async XLA Ops:
  2.1 28.5 %copy-start.3 = (bf16[1,2,64,2,2048]{4,3,2,1,0:T(2,128)(2,1)S(1)}, bf16[1,2,64,2,2048]{4,3,2,1,0:T(2,128)(2,1)}, u32[]{:S(2)}) copy-start(bf16[1,2,64,2,2048]{4,3,2,1,0:T(2,128)(2,1)} %param.13) | copy-start | bytes 3145732
  2.3 48.5 %collective-permute-start = (bf16[32,2,2048]{2,1,0:T(2,128)(2,1)S(1)}, bf16[32,2,2048]{2,1,0:T(2,128)(2,1)S(1)}, u32[]{:S(2)}, u32[]{:S(2)}) collective-permute-start(bf16[32,2,2048]{2,1,0:T(2,128)(2,1)S(1)} %dynamic-slice_bitcast_fusion), channel_id=1, source_target_pairs={{0,22},{1,23},{2,20},{3,21},{4,18},{5,19},{6,16},{7,17},{8,14},{9,... | collective-permute-start | bytes 786440 | tf_op jit(solution)/shard_map/ppermute | solution.py:36
  20.3 46.8 %all-to-all-start = ((bf16[64,24,256]{2,1,0:T(8,128)(2,1)}), bf16[64,24,256]{2,1,0:T(8,128)(2,1)S(1)}, u32[]{:S(2)}, u32[]{:S(2)}) async-start(bf16[64,24,256]{2,1,0:T(8,128)(2,1)} %bitcast.20), calls=%async_computation | async-start | bytes 1572864 | tf_op jit(solution)/shard_map/all_to_all | solution.py:43
  67.1 4.6 %copy-start.2 = (bf16[64,24,256]{2,1,0:T(8,128)(2,1)}, bf16[64,24,256]{2,1,0:T(8,128)(2,1)S(1)}, u32[]{:S(2)}) copy-start(bf16[64,24,256]{2,1,0:T(8,128)(2,1)S(1)} %all-to-all-done) | copy-start | bytes 2359300
  67.1 4.6 %collective-permute-start.1 = (bf16[1536,256]{1,0:T(8,128)(2,1)S(1)}, bf16[1536,256]{1,0:T(8,128)(2,1)S(1)}, u32[]{:S(2)}, u32[]{:S(2)}) collective-permute-start(bf16[1536,256]{1,0:T(8,128)(2,1)S(1)} %bitcast.18), channel_id=1, source_target_pairs={{0,1},{1,0},{2,3},{3,2},{4,5},{5,4},{6,7},{7,6},{8,9},{9,8},{10,11... | collective-permute-start | bytes 2359304 | tf_op jit(solution)/shard_map/ppermute | solution.py:20
  71.7 0.9 copy-start.4
  77.3 4.0 %collective-permute-start.2 = (bf16[256,1024]{1,0:T(8,128)(2,1)}, bf16[256,1024]{1,0:T(8,128)(2,1)S(1)}, u32[]{:S(2)}, u32[]{:S(2)}) collective-permute-start(bf16[256,1024]{1,0:T(8,128)(2,1)} %get-tuple-element.34), channel_id=1, source_target_pairs={{0,1},{1,0},{2,3},{3,2},{4,5},{5,4},{6,7},{7,6},{8,9},{9,8},{10,11... | collective-permute-start | bytes 1572872 | tf_op jit(solution)/shard_map/ppermute | solution.py:20
  81.3 1.2 copy-start
  83.7 23.8 %all-to-all-start.1 = ((bf16[64,16,256]{2,1,0:T(8,128)(2,1)}), bf16[64,16,256]{2,1,0:T(8,128)(2,1)S(1)}, u32[]{:S(2)}, u32[]{:S(2)}) async-start(bf16[64,16,256]{2,1,0:T(8,128)(2,1)} %bitcast.9), calls=%async_computation.1 | async-start | bytes 1048576 | tf_op jit(solution)/shard_map/all_to_all | solution.py:43
  90.8 3.7 %collective-permute-start.3 = (bf16[32,2,2048]{2,1,0:T(2,128)(2,1)S(1)}, bf16[32,2,2048]{2,1,0:T(2,128)(2,1)S(1)}, u32[]{:S(2)}, u32[]{:S(2)}) collective-permute-start(bf16[32,2,2048]{2,1,0:T(2,128)(2,1)S(1)} %collective-permute-done), channel_id=1, source_target_pairs={{0,1},{1,0},{2,3},{3,2},{4,5},{5,4},{6,7},{7,6},{8,9},{9,8},{10,11... | collective-permute-start | bytes 786440 | tf_op jit(solution)/shard_map/ppermute | solution.py:20
  95.3 12.2 %copy-start.1 = (bf16[256,16]{1,0:T(8,128)(2,1)S(1)}, bf16[256,16]{1,0:T(8,128)(2,1)}, u32[]{:S(2)}) copy-start(bf16[256,16]{1,0:T(8,128)(2,1)} %get-tuple-element.42.place) | copy-start | bytes 24580
  108.0 4.7 %collective-permute-start.4 = (bf16[16,1024]{1,0:T(8,128)(2,1)S(1)}, bf16[16,1024]{1,0:T(8,128)(2,1)S(1)}, u32[]{:S(2)}, u32[]{:S(2)}) collective-permute-start(bf16[16,1024]{1,0:T(8,128)(2,1)S(1)} %get-tuple-element.44), channel_id=1, source_target_pairs={{0,2},{1,3},{2,0},{3,1},{4,6},{5,7},{6,4},{7,5},{8,10},{9,11},{10,... | collective-permute-start | bytes 98312 | tf_op jit(solution)/shard_map/ppermute | solution.py:20
  112.7 6.2 %collective-permute-start.6 = (bf16[16,1024]{1,0:T(8,128)(2,1)S(1)}, bf16[16,1024]{1,0:T(8,128)(2,1)S(1)}, u32[]{:S(2)}, u32[]{:S(2)}) collective-permute-start(bf16[16,1024]{1,0:T(8,128)(2,1)S(1)} %fusion), channel_id=1, source_target_pairs={{0,8},{1,9},{2,10},{3,11},{4,0},{5,1},{6,2},{7,3},{8,4},{9,5},{10,... | collective-permute-start | bytes 98312 | tf_op jit(solution)/shard_map/ppermute | solution.py:20
  114.6 8.9 %collective-permute-start.5 = (bf16[16,1024]{1,0:T(8,128)(2,1)S(1)}, bf16[16,1024]{1,0:T(8,128)(2,1)S(1)}, u32[]{:S(2)}, u32[]{:S(2)}) collective-permute-start(bf16[16,1024]{1,0:T(8,128)(2,1)S(1)} %fusion), channel_id=1, source_target_pairs={{0,4},{1,5},{2,6},{3,7},{4,8},{5,9},{6,10},{7,11},{8,0},{9,1},{10,... | collective-permute-start | bytes 98312 | tf_op jit(solution)/shard_map/ppermute | solution.py:20
  123.5 5.7 %collective-permute-start.7 = (bf16[16,1024]{1,0:T(8,128)(2,1)S(1)}, bf16[16,1024]{1,0:T(8,128)(2,1)S(1)}, u32[]{:S(2)}, u32[]{:S(2)}) collective-permute-start(bf16[16,1024]{1,0:T(8,128)(2,1)S(1)} %add_convert_fusion.own), channel_id=1, source_target_pairs={{0,1},{1,0},{2,3},{3,2},{4,5},{5,4},{6,7},{7,6},{8,9},{9,8},{10,11... | collective-permute-start | bytes 98312 | tf_op jit(solution)/shard_map/ppermute | solution.py:20

commit v3 on v2

--- a/solution.py
+++ b/solution.py
@@ -107,7 +107,8 @@
     return jnp.concatenate(parts)
 
 
-def prep_kernel(routes, probs, out_grad, outgoing):
+def prep_kernel(routes, probs, out_grad, outgoing_out, outgoing, sems):
+    stores = []
     half = out_grad[:, half_at(lax.axis_index("dp") % 2)]
     table = by_slot()
     _, rows = routed(slots(), routes, probs, half)
@@ -122,6 +123,13 @@
                 at = 24 * (16 * g + 8 * h + c)
                 outgoing[at : at + 16, :] = held[h][16 * c : 16 * c + 16, :]
                 outgoing[at + 16 : at + 24, :] = extra[64 * h + 8 * c : 64 * h + 8 * c + 8, :]
+        done = pl.ds(384 * g, 384)
+        stores.append(
+            pltpu.make_async_copy(outgoing.at[done], outgoing_out.at[done], sems.at[g])
+        )
+        stores[g].start()
+    for store in stores:
+        store.wait()
 
 
 def act(x, w_gate, w_up):
@@ -133,98 +141,144 @@
     return active, slope, (active * up).astype(BF)
 
 
-def act_kernel(x, home_gu, spare_gu, routes, active, slope, hidden, place_out):
+def act_kernel(x, home_gu, spare_gu, routes, acts, hidden, place_out):
     for p, place in enumerate(places_of(slots(), routes)):
         place_out[128 * p : 128 * p + 128, :] = place.astype(BF)
     for j, w in enumerate((home_gu, spare_gu)):
-        a, s, h = act(x[128 * j : 128 * j + 128, :], w[0], w[1])
-        active[128 * j : 128 * j + 128, :] = a
-        slope[128 * j : 128 * j + 128, :] = s
+        active, slope, h = act(x[128 * j : 128 * j + 128, :], w[0], w[1])
+        acts[128 * j : 128 * j + 128, :] = active
+        acts[256 + 128 * j : 256 + 128 * j + 128, :] = slope
         hidden[128 * j : 128 * j + 128, :] = h
 
 
-def rows_kernel(
-    own_in,
-    other_in,
-    active_in,
-    slope_in,
-    home_d,
-    spare_d,
-    home_gu,
-    spare_gu,
-    sent_out,
-    kept_out,
-    grads_out,
-    block_out,
-    got,
-    active,
-    slope,
-    w_d,
-    w_gu,
-    block,
-    sent,
-    kept,
-    grads,
-    sems,
-    out_sems,
+def pack_kernel(home_d, spare_d, home_gu, spare_gu, packed_out, packed, sems):
+    there = 1024 * (1 - lax.axis_index("dp") % 2)
+    rows = pl.ds(pl.multiple_of(there, 1024), 1024)
+    copies = []
+    for j, (w_d, w_gu) in enumerate(((home_d, home_gu), (spare_d, spare_gu))):
+        for i in range(2):
+            copies.append((w_gu.at[i, rows], packed.at[pl.ds(3072 * j + 1024 * i, 1024)]))
+        for b in range(8):
+            cols = pl.ds(pl.multiple_of(there + 128 * b, 128), 128)
+            to = packed.at[pl.ds(3072 * j + 2048 + 128 * b, 128)]
+            copies.append((w_d.at[:, cols], to))
+    copies = [pltpu.make_async_copy(c[0], c[1], sems.at[i]) for i, c in enumerate(copies)]
+    for copy in copies:
+        copy.start()
+    for copy in copies:
+        copy.wait()
+    store = pltpu.make_async_copy(packed, packed_out, sems.at[20])
+    store.start()
+    store.wait()
+
+
+def sorted_rows(table, got, g):
+    rows = dot(table, got[192 * g : 192 * g + 192, :]).astype(BF)
+    for j in range(3):
+        parts = [rows[64 * j + 16 * f : 64 * j + 16 * f + 16, :] for f in range(4)]
+        yield 128 * j + 16 * g, jnp.concatenate(parts, axis=1)
+
+
+def hidden_kernel(
+    own_in, home_d, spare_d, packed, part_out, block_out, got, w_d, w_there, part, block, sems, outs
 ):
-    core = lax.axis_index("dp") % 2
-    here, there = half_at(core), half_at(1 - core)
-    pairs = [
-        (own_in, got.at[0]),
-        (other_in, got.at[1]),
-        (home_d, w_d.at[0]),
-        (slope_in, slope),
-        (active_in, active),
-        (home_gu, w_gu.at[0]),
-        (spare_d, w_d.at[1]),
-        (spare_gu, w_gu.at[1]),
-    ]
+    here = half_at(lax.axis_index("dp") % 2)
+    pairs = [(own_in, got)]
+    for j, w in enumerate((home_d, spare_d)):
+        pairs.append((w.at[:, here], w_d.at[j]))
+        pairs.append((packed.at[pl.ds(3072 * j + 2048, 1024)], w_there.at[j]))
     loads = [pltpu.make_async_copy(a, b, sems.at[i]) for i, (a, b) in enumerate(pairs)]
     for load in loads:
         load.start()
     table = by_source(3)
-    for i, at in enumerate((here, there)):
-        loads[i].wait()
-        for g in range(GROUPS):
-            rows = dot(table, got[i, 192 * g : 192 * g + 192, :]).astype(BF)
-            for j in range(3):
-                parts = [rows[64 * j + 16 * f : 64 * j + 16 * f + 16, :] for f in range(4)]
-                block[128 * j + 16 * g : 128 * j + 16 * g + 16, at] = jnp.concatenate(parts, axis=1)
-    stores = [pltpu.make_async_copy(block, block_out, out_sems.at[0])]
-    stores[0].start()
+    loads[0].wait()
+    for g in range(GROUPS):
+        for at, rows in sorted_rows(table, got, g):
+            block[at : at + 16, :] = rows
+    store = pltpu.make_async_copy(block, block_out, outs.at[0])
+    store.start()
+    for load in loads[1:]:
+        load.wait()
+    for j in range(2):
+        mine = slice(128 * j, 128 * j + 128)
+        there = [w_there[j, 128 * b : 128 * b + 128, :] for b in range(8)]
+        weights = jnp.concatenate([w_d[j], jnp.concatenate(there, axis=1)])
+        part[mine, :] = dot(block[mine, :], weights, NT)
+    last = pltpu.make_async_copy(part, part_out, outs.at[1])
+    last.start()
+    last.wait()
+    store.wait()
+
+
+def rows_kernel(
+    part_in,
+    part_got,
+    acts_in,
+    acts_got,
+    home_gu,
+    spare_gu,
+    packed,
+    outgoing_out,
+    grads_out,
+    part,
+    acts,
+    w_gu,
+    grads,
+    rows,
+    outgoing,
+    sems,
+    outs,
+):
+    here = half_at(lax.axis_index("dp") % 2)
+    pairs = [
+        (part_in, part.at[0]),
+        (part_got, part.at[1]),
+        (acts_in, acts.at[0]),
+        (acts_got, acts.at[1]),
+    ]
+    for j, w in enumerate((home_gu, spare_gu)):
+        for i in range(2):
+            pairs.append((w.at[i, here], w_gu.at[j, i]))
+            pairs.append((packed.at[pl.ds(3072 * j + 1024 * i, 1024)], w_gu.at[j, 2 + i]))
+    loads = [pltpu.make_async_copy(a, b, sems.at[i]) for i, (a, b) in enumerate(pairs)]
+    for load in loads:
+        load.start()
+    for load in loads[:4]:
+        load.wait()
     for j in range(2):
         mine = pl.ds(128 * j, 128)
-        for i in ((2, 3, 4) if j == 0 else (6,)):
-            loads[i].wait()
-        hidden_grad = dot(block[mine, :], w_d[j], NT)
-        both = jnp.concatenate(
-            [(hidden_grad * slope[mine, :]).astype(BF), (hidden_grad * active[mine, :]).astype(BF)],
-            axis=1,
-        )
-        grads[mine, :] = both
-        loads[5 if j == 0 else 7].wait()
-        weights = jnp.concatenate([w_gu[j, 0, here, :], w_gu[j, 1, here, :]], axis=1)
-        kept[mine, :] = dot(both, weights, NT)
-        weights = jnp.concatenate([w_gu[j, 0, there, :], w_gu[j, 1, there, :]], axis=1)
-        sent[mine, :] = dot(both, weights, NT).astype(BF)
-        for i, (a, b) in enumerate(((kept, kept_out), (sent, sent_out), (grads, grads_out))):
-            store = pltpu.make_async_copy(a.at[mine], b.at[mine], out_sems.at[1 + 3 * j + i])
-            store.start()
-            stores.append(store)
-    for store in stores:
-        store.wait()
-
-
-def pair_kernel(kept, got, outgoing):
+        slopes = pl.ds(256 + 128 * j, 128)
+        both = []
+        for k in range(2):
+            hidden_grad = (
+                part[0, mine, 128 * k : 128 * k + 128]
+                + part[1, mine, 128 - 128 * k : 256 - 128 * k]
+            )
+            both.append((hidden_grad * acts[k, slopes, :]).astype(BF))
+            both.append((hidden_grad * acts[k, mine, :]).astype(BF))
+        grads[mine, :] = jnp.concatenate(both[:2], axis=1)
+        for load in loads[4 + 4 * j : 8 + 4 * j]:
+            load.wait()
+        weights = jnp.concatenate([w_gu[j, i] for i in (0, 1, 2, 3)], axis=1)
+        rows[mine, :] = dot(jnp.concatenate(both, axis=1), weights, NT).astype(BF)
+    stores = [pltpu.make_async_copy(grads, grads_out, outs.at[0])]
+    stores[0].start()
     table = by_source(2)
     for g in range(GROUPS):
         parts = []
         for j in range(2):
             at = slice(128 * j + 16 * g, 128 * j + 16 * g + 16)
-            total = (kept[at, :] + got[at, :].astype(F32)).astype(BF)
-            parts += [total[:, 256 * f : 256 * f + 256] for f in range(4)]
+            parts += [rows[at, 256 * f : 256 * f + 256] for f in range(4)]
         outgoing[128 * g : 128 * g + 128, :] = dot(table, jnp.concatenate(parts), TN).astype(BF)
+        if g % 4 == 3:
+            done = pl.ds(128 * (g - 3), 512)
+            store = pltpu.make_async_copy(
+                outgoing.at[done], outgoing_out.at[done], outs.at[1 + g // 4]
+            )
+            store.start()
+            stores.append(store)
+    for store in stores:
+        store.wait()
 
 
 def combine_kernel(returned, place, mine, low, rows):
@@ -245,7 +299,8 @@
     x,
     x_own,
     x_other,
-    block,
+    block_own,
+    other,
     grads,
     hidden,
     home_gu,
@@ -253,8 +308,14 @@
     grad_gu,
     grad_d,
     x_prior,
+    block,
 ):
     core = lax.axis_index("dp") % 2
+    block[:, half_at(core)] = block_own[...]
+    table = by_source(3)
+    for g in range(GROUPS):
+        for at, rows in sorted_rows(table, other, g):
+            block[at : at + 16, half_at(1 - core)] = rows
     x_prior[pl.ds(pl.multiple_of(64 * core, 64), 64), :] = x_own[...]
     x_prior[pl.ds(pl.multiple_of(64 - 64 * core, 64), 64), :] = x_other[...]
     column = lax.axis_index("ep")
@@ -325,72 +386,94 @@
     x_part, routes, route_probs = lax.optimization_barrier((x_part, routes, route_probs))
     x_part = to_next(x_part)
 
-    outgoing = call(prep_kernel, shape((1536, 256)), 10**6, 10**6, [VMEM] * 3)(
-        routes.T, route_probs.T, out_grad
-    )
+    outgoing = call(
+        prep_kernel,
+        shape((1536, 256)),
+        10**6,
+        10**6,
+        [VMEM] * 3,
+        [pltpu.VMEM((1536, 256), BF), pltpu.SemaphoreType.DMA((4,))],
+        ANY,
+    )(routes.T, route_probs.T, out_grad)
     incoming = exchange(outgoing)
 
     saved, _ = lax.optimization_barrier((saved_inputs, outgoing))
     x = saved.reshape(256, 2048)
-    active, slope, hidden, place = call(
+    acts, hidden, place = call(
         act_kernel,
-        (
-            shape((256, 128), F32),
-            shape((256, 128), F32),
-            shape((256, 128)),
-            shape((256, 16)),
-        ),
+        (shape((512, 128), F32), shape((256, 128)), shape((256, 16))),
         10**11,
         4 * 10**6,
         [VMEM] * 4,
     )(x, home_gu, spare_gu, routes.T)
-    incoming, active, x_part = lax.optimization_barrier((incoming, active, x_part))
-
-    other = swap_cores(incoming)
-    sent, kept, grads, block = call(
+    weights, _ = lax.optimization_barrier(((home_d, spare_d, home_gu, spare_gu), outgoing))
+    packed = call(
+        pack_kernel,
+        shape((6144, 128)),
+        10**6,
+        10**6,
+        [ANY] * 4,
+        [pltpu.VMEM((6144, 128), BF), pltpu.SemaphoreType.DMA((21,))],
+        ANY,
+    )(*weights)
+    packed = swap_cores(packed)
+    acts_got = swap_cores(acts)
+    incoming, acts, x_part, packed, acts_got = lax.optimization_barrier(
+        (incoming, acts, x_part, packed, acts_got)
+    )
+
+    part, block_own = call(
+        hidden_kernel,
+        (shape((256, 256), F32), shape((384, 1024))),
+        10**9,
+        4 * 10**6,
+        [ANY] * 4,
+        [
+            pltpu.VMEM((1536, 256), BF),
+            pltpu.VMEM((2, 128, 1024), BF),
+            pltpu.VMEM((2, 1024, 128), BF),
+            pltpu.VMEM((256, 256), F32),
+            pltpu.VMEM((384, 1024), BF),
+            pltpu.SemaphoreType.DMA((5,)),
+            pltpu.SemaphoreType.DMA((2,)),
+        ],
+        (ANY, ANY),
+    )(incoming, home_d, spare_d, packed)
+    pair, grads = call(
         rows_kernel,
-        (
-            shape((256, 1024)),
-            shape((256, 1024), F32),
-            shape((256, 256)),
-            shape((384, 2048)),
-        ),
+        (shape((1024, 256)), shape((256, 256))),
         10**9,
-        8 * 10**6,
-        [ANY] * 8,
+        4 * 10**6,
+        [ANY] * 7,
         [
-            pltpu.VMEM((2, 1536, 256), BF),
-            pltpu.VMEM((256, 128), F32),
-            pltpu.VMEM((256, 128), F32),
-            pltpu.VMEM((2, 128, 2048), BF),
-            pltpu.VMEM((2, 2, 2048, 128), BF),
-            pltpu.VMEM((384, 2048), BF),
+            pltpu.VMEM((2, 256, 256), F32),
+            pltpu.VMEM((2, 512, 128), F32),
+            pltpu.VMEM((2, 4, 1024, 128), BF),
+            pltpu.VMEM((256, 256), BF),
             pltpu.VMEM((256, 1024), BF),
-            pltpu.VMEM((256, 1024), F32),
-            pltpu.VMEM((256, 256), BF),
-            pltpu.SemaphoreType.DMA((8,)),
-            pltpu.SemaphoreType.DMA((7,)),
+            pltpu.VMEM((1024, 256), BF),
+            pltpu.SemaphoreType.DMA((12,)),
+            pltpu.SemaphoreType.DMA((3,)),
         ],
-        (ANY, ANY, ANY, ANY),
-    )(incoming, other, active, slope, home_d, spare_d, home_gu, spare_gu)
-    got = swap_cores(sent)
-    pair = call(pair_kernel, shape((1024, 256)), 10**8, 2 * 10**6, [VMEM] * 2, vmem=28)(kept, got)
+        (ANY, ANY),
+    )(part, swap_cores(part), acts, acts_got, home_gu, spare_gu, packed)
     returned = exchange(pair)
 
-    x_part, _ = lax.optimization_barrier((x_part, pair))
+    x_part, incoming, _ = lax.optimization_barrier((x_part, incoming, pair))
     grad_gu, grad_d = call(
         weights_kernel,
         (shape((2, 2048, 128)), shape((128, 2048))),
         10**8,
         10**6,
-        [SMEM] + [VMEM] * 8,
-        [pltpu.VMEM((128, 2048), BF)],
+        [SMEM] + [VMEM] * 9,
+        [pltpu.VMEM((128, 2048), BF), pltpu.VMEM((384, 2048), BF)],
     )(
         replica_expert,
         x,
         x_part.reshape(64, 2048),
         swap_cores(x_part).reshape(64, 2048),
-        block,
+        block_own,
+        swap_cores(incoming),
         grads,
         hidden,
         home_gu,
@@ -407,11 +490,10 @@
         [pltpu.VMEM((256, 1024), BF)],
         vmem=28,
     )(returned, place)
-    total = mine + along_dp(low, lambda z: (z ^ 1, 0)).astype(F32)
-    low = total.astype(BF)
-    one = along_dp(low, lambda z: ((z + 2) % 6, 0))
-    two = along_dp(low, lambda z: ((z + 4) % 6, 0))
-    total = (total + one.astype(F32) + two.astype(F32)).astype(BF)
+    one = along_dp(low, lambda z: (z // 3 * 3 + (z + 1) % 3, 0))
+    two = along_dp(low, lambda z: (z // 3 * 3 + (z + 2) % 3, 0))
+    total = mine + one.astype(F32) + two.astype(F32)
+    total = (total + along_dp(total.astype(BF), lambda z: ((z + 3) % 6, 0)).astype(F32)).astype(BF)
     input_grad = call(finish_kernel, shape((16, 2048)), 10**3, 10**5, [VMEM] * 2, vmem=28)(
         total, swap_cores(total)
     )

time: 130 us -> 125 us (0.962)
  waiting for transfers between devices: 51.2 us -> 34.4 us
  starting transfers between devices: 53.1 us -> 59.2 us
  Pallas kernels: 18.1 us -> 21.5 us
  local copies, waits for them, and re-layouts: 6.53 us -> 8.59 us
    ppermute x1, waiting for transfers between devices: 15.7 us -> 8.1 us  [to_next(): return lax.ppermute(array, ('ep', 'dp'), pairs)]
    ppermute x7 -> x9, starting transfers between devices: 20.5 us -> 26.7 us  [along_dp(): return lax.ppermute(array, 'dp', pairs)]
    ppermute x7 -> x9, waiting for transfers between devices: 12.2 us -> 6.97 us  [along_dp(): return lax.ppermute(array, 'dp', pairs)]
    all_to_all x2, waiting for transfers between devices: 23.4 us -> 19.3 us  [exchange(): lax.all_to_all(array, ('ep', 'dp'), split_axis=0, concat_axis=0, axis_ind...]
    pallas_call x4 -> x5, Pallas kernels: 11.9 us -> 15.1 us  [the longest x1 3.57 us: on_device(): call(rows_kernel, (shape((1024, 256)), shape((256, 256))), 10 ** 9, 4 * 1...]
  transfers between devices with their start and end apart: 10 -> 12, of which waited for: 9 -> 7; matrix products, arithmetic and copies ran while one was open for 2% -> 3% of each run, Pallas kernels for 9% -> 11%
where the time goes in v3:
time: 125 us
  starting transfers between devices  59.2 us (47%)
  waiting for transfers between devices  34.4 us (28%)
  Pallas kernels  21.5 us (17%)
  local copies, waits for them, and re-layouts  8.59 us (7%)
    ppermute x9, starting transfers between devices, along_dp(): return lax.ppermute(array, 'dp', pairs)  26.7 us
    all_to_all x2, waiting for transfers between devices, exchange(): lax.all_to_all(array, ('ep', 'dp'), split_axis=0, concat_axis=0, axis_ind...  19.3 us
    all_to_all x2, starting transfers between devices, exchange(): lax.all_to_all(array, ('ep', 'dp'), split_axis=0, concat_axis=0, axis_ind...  16.7 us
    ppermute x1, starting transfers between devices, to_next(): return lax.ppermute(array, ('ep', 'dp'), pairs)  15.8 us
    ppermute x1, waiting for transfers between devices, to_next(): return lax.ppermute(array, ('ep', 'dp'), pairs)  8.1 us
    ppermute x9, waiting for transfers between devices, along_dp(): return lax.ppermute(array, 'dp', pairs)  6.97 us
    pallas_call x1, Pallas kernels, on_device(): call(weights_kernel, (shape((2, 2048, 128)), shape((128, 2048))), 10 ** 8...  5.37 us
    pallas_call x1, Pallas kernels, on_device(): call(rows_kernel, (shape((1024, 256)), shape((256, 256))), 10 ** 9, 4 * 1...  3.57 us
  transfers between devices with their start and end apart: 12, of which 7 were waited for; matrix products, arithmetic and copies ran while one was open for 3% of the time, Pallas kernels for 11%

profile of v3, /device:TPU:1, one launch (start us, length us, event | category | flops | bytes accessed | tf_op | source)
XLA Modules:
  0.0 124.7 jit_solution(6099559215108995134)
XLA Ops:
  0.7 1.4 %slice.3 = bf16[1,1,64,2,2048]{4,3,2,1,0:T(2,128)(2,1)S(1)} slice(bf16[1,2,64,2,2048]{4,3,2,1,0:T(2,128)(2,1)} %param.13), slice={[0:1], [1:2], [0:64], [0:2], [0:2048]} | slice | bytes 1048576 | tf_op jit(solution)/shard_map/slice | solution.py:385
  2.1 0.9 dynamic-slice_bitcast_fusion
  3.0 15.8 %collective-permute-start = (bf16[32,2,2048]{2,1,0:T(2,128)(2,1)}, bf16[32,2,2048]{2,1,0:T(2,128)(2,1)}, u32[]{:S(2)}, u32[]{:S(2)}) collective-permute-start(bf16[32,2,2048]{2,1,0:T(2,128)(2,1)} %dynamic-slice_bitcast_fusion), channel_id=1, source_target_pairs={{0,22},{1,23},{2,20},{3,21},{4,18},{5,19},{6,16},{7,17},{8,14},{9,... | collective-permute-start | bytes 786440 | tf_op jit(solution)/shard_map/ppermute | solution.py:36
  18.8 2.6 %shard_map.112 = bf16[1536,256]{1,0:T(8,128)(2,1)} custom-call(s32[8,16]{1,0:T(8,128)} %bitcast.32, f32[8,16]{1,0:T(8,128)} %bitcast.31, bf16[16,2048]{1,0:T(8,128)(2,1)} %out_grad.1), custom_call_target="tpu_custom_call" | custom-call | flops 1000000 | bytes 1000000 | tf_op jit(solution)/shard_map/pallas_call | solution.py:389
  21.4 9.6 %all-to-all-start = ((bf16[64,24,256]{2,1,0:T(8,128)(2,1)}), bf16[64,24,256]{2,1,0:T(8,128)(2,1)S(1)}, u32[]{:S(2)}, u32[]{:S(2)}) async-start(bf16[64,24,256]{2,1,0:T(8,128)(2,1)} %bitcast.22), calls=%async_computation | async-start | bytes 1572864 | tf_op jit(solution)/shard_map/all_to_all | solution.py:43
  31.0 2.8 %shard_map.114 = bf16[6144,128]{1,0:T(8,128)(2,1)} custom-call(bf16[128,2048]{1,0:T(8,128)(2,1)} %bitcast.23, bf16[128,2048]{1,0:T(8,128)(2,1)} %bitcast.28, bf16[2,2048,128]{2,1,0:T(8,128)(2,1)} %bitcast.15, bf16[2,2048,128]{2,1,0:T(8,128)(2,1)} %bitcast.19), custom_call_target="tpu_custom_call" | custom-call | flops 1000000 | bytes 1000000 | tf_op jit(solution)/shard_map/pallas_call | solution.py:410
  33.8 3.1 %collective-permute-start.1 = (bf16[6144,128]{1,0:T(8,128)(2,1)}, bf16[6144,128]{1,0:T(8,128)(2,1)S(1)}, u32[]{:S(2)}, u32[]{:S(2)}) collective-permute-start(bf16[6144,128]{1,0:T(8,128)(2,1)} %shard_map.114), channel_id=1, source_target_pairs={{0,1},{1,0},{2,3},{3,2},{4,5},{5,4},{6,7},{7,6},{8,9},{9,8},{10,11... | collective-permute-start | bytes 4718600 | tf_op jit(solution)/shard_map/ppermute | solution.py:20
  37.0 1.2 reshape.30.x
  38.2 3.4 %shard_map.113 = (f32[512,128]{1,0:T(8,128)}, bf16[256,128]{1,0:T(8,128)(2,1)}, bf16[256,16]{1,0:T(8,128)(2,1)}) custom-call(bf16[256,2048]{1,0:T(8,128)(2,1)} %reshape.30.x, bf16[2,2048,128]{2,1,0:T(8,128)(2,1)} %bitcast.16, bf16[2,2048,128]{2,1,0:T(8,128)(2,1)} %bitcast.20, s32[8,16]{1,0:T(8,128)} %bitcast.33), custom_call_target="tpu_custom_call" | custom-call | flops 99999997952 | bytes 4000000 | tf_op jit(solution)/shard_map/pallas_call | solution.py:402
  41.6 1.9 %collective-permute-start.2 = (f32[512,128]{1,0:T(8,128)}, f32[512,128]{1,0:T(8,128)S(1)}, u32[]{:S(2)}, u32[]{:S(2)}) collective-permute-start(f32[512,128]{1,0:T(8,128)} %get-tuple-element.43.acts_in), channel_id=1, source_target_pairs={{0,1},{1,0},{2,3},{3,2},{4,5},{5,4},{6,7},{7,6},{8,9},{9,8},{10,11... | collective-permute-start | bytes 786440 | tf_op jit(solution)/shard_map/ppermute | solution.py:20
  43.5 8.1 %collective-permute-done = bf16[32,2,2048]{2,1,0:T(2,128)(2,1)} collective-permute-done((bf16[32,2,2048]{2,1,0:T(2,128)(2,1)}, bf16[32,2,2048]{2,1,0:T(2,128)(2,1)}, u32[]{:S(2)}, u32[]{:S(2)}) %collective-permute-start) | collective-permute-done | bytes 262176 | tf_op jit(solution)/shard_map/ppermute | solution.py:36
  51.6 16.3 %all-to-all-done = bf16[64,24,256]{2,1,0:T(8,128)(2,1)S(1)} async-done(((bf16[64,24,256]{2,1,0:T(8,128)(2,1)}), bf16[64,24,256]{2,1,0:T(8,128)(2,1)S(1)}, u32[]{:S(2)}, u32[]{:S(2)}) %all-to-all-start) | async-done | bytes 786464 | tf_op jit(solution)/shard_map/all_to_all | solution.py:43
  67.9 0.9 copy-done.4
  68.8 2.7 %shard_map.115 = (f32[256,256]{1,0:T(8,128)}, bf16[384,1024]{1,0:T(8,128)(2,1)}) custom-call(bf16[1536,256]{1,0:T(8,128)(2,1)} %bitcast.26, bf16[128,2048]{1,0:T(8,128)(2,1)} %bitcast.24, bf16[128,2048]{1,0:T(8,128)(2,1)} %bitcast.29, bf16[6144,128]{1,0:T(8,128)(2,1)} %copy-done.2), custom_call_target="tpu_custom_call" | custom-call | flops 1000000000 | bytes 4000000 | tf_op jit(solution)/shard_map/pallas_call | solution.py:425
  71.5 2.8 %collective-permute-start.3 = (f32[256,256]{1,0:T(8,128)}, f32[256,256]{1,0:T(8,128)S(1)}, u32[]{:S(2)}, u32[]{:S(2)}) collective-permute-start(f32[256,256]{1,0:T(8,128)} %get-tuple-element.42.part_in), channel_id=1, source_target_pairs={{0,1},{1,0},{2,3},{3,2},{4,5},{5,4},{6,7},{7,6},{8,9},{9,8},{10,11... | collective-permute-start | bytes 786440 | tf_op jit(solution)/shard_map/ppermute | solution.py:20
  74.3 1.4 %collective-permute-done.3.part_got = f32[256,256]{1,0:T(8,128)S(1)} collective-permute-done((f32[256,256]{1,0:T(8,128)}, f32[256,256]{1,0:T(8,128)S(1)}, u32[]{:S(2)}, u32[]{:S(2)}) %collective-permute-start.3) | collective-permute-done | bytes 262176 | tf_op jit(solution)/shard_map/ppermute | solution.py:20
  76.4 3.6 %shard_map.116 = (bf16[1024,256]{1,0:T(8,128)(2,1)}, bf16[256,256]{1,0:T(8,128)(2,1)}) custom-call(f32[256,256]{1,0:T(8,128)} %get-tuple-element.42.part_in, f32[256,256]{1,0:T(8,128)} %copy-done.7, f32[512,128]{1,0:T(8,128)} %get-tuple-element.43.acts_in, f32[512,128]{1,0:T(8,128)} %copy-done.6, bf16[2,2048,128]{2,1,0:T(8,128)(2,1)} %bitcast.17, ...), custom_call_target="tpu_custom_call" | custom-call | flops 1000000000 | bytes 4000000 | tf_op jit(solution)/shard_map/pallas_call | solution.py:442
  80.0 7.1 %all-to-all-start.1 = ((bf16[64,16,256]{2,1,0:T(8,128)(2,1)}), bf16[64,16,256]{2,1,0:T(8,128)(2,1)S(1)}, u32[]{:S(2)}, u32[]{:S(2)}) async-start(bf16[64,16,256]{2,1,0:T(8,128)(2,1)} %bitcast.30), calls=%async_computation.1 | async-start | bytes 1048576 | tf_op jit(solution)/shard_map/all_to_all | solution.py:43
  87.1 2.6 %collective-permute-start.5 = (bf16[1536,256]{1,0:T(8,128)(2,1)S(1)}, bf16[1536,256]{1,0:T(8,128)(2,1)S(1)}, u32[]{:S(2)}, u32[]{:S(2)}) collective-permute-start(bf16[1536,256]{1,0:T(8,128)(2,1)S(1)} %bitcast.27), channel_id=1, source_target_pairs={{0,1},{1,0},{2,3},{3,2},{4,5},{5,4},{6,7},{7,6},{8,9},{9,8},{10,11... | collective-permute-start | bytes 2359304 | tf_op jit(solution)/shard_map/ppermute | solution.py:20
  89.7 1.9 %collective-permute-start.4 = (bf16[32,2,2048]{2,1,0:T(2,128)(2,1)}, bf16[32,2,2048]{2,1,0:T(2,128)(2,1)S(1)}, u32[]{:S(2)}, u32[]{:S(2)}) collective-permute-start(bf16[32,2,2048]{2,1,0:T(2,128)(2,1)} %collective-permute-done), channel_id=1, source_target_pairs={{0,1},{1,0},{2,3},{3,2},{4,5},{5,4},{6,7},{7,6},{8,9},{9,8},{10,11... | collective-permute-start | bytes 786440 | tf_op jit(solution)/shard_map/ppermute | solution.py:20
  91.6 1.8 %reshape.33.x_own = bf16[64,2048]{1,0:T(8,128)(2,1)} reshape(bf16[32,2,2048]{2,1,0:T(2,128)(2,1)} %collective-permute-done) | data formatting | bytes 524288 | tf_op jit(solution)/shard_map/reshape | solution.py:473
  93.3 0.8 reshape.34.x_other
  94.2 0.9 copy-done.3
  95.1 5.4 %shard_map.117 = (bf16[2,2048,128]{2,1,0:T(8,128)(2,1)}, bf16[128,2048]{1,0:T(8,128)(2,1)}) custom-call(s32[64]{0:T(128)} %experts.1, bf16[256,2048]{1,0:T(8,128)(2,1)} %reshape.30.x, bf16[64,2048]{1,0:T(8,128)(2,1)} %reshape.33.x_own, bf16[64,2048]{1,0:T(8,128)(2,1)} %reshape.34.x_other, bf16[384,1024]{1,0:T(8,128)(2,1)} %get-tuple-element.48.block_own, ...), custom_call_target="tpu_custom_call" | custom-call | flops 100000000 | bytes 1000000 | tf_op jit(solution)/shard_map/pallas_call | solution.py:463
  100.4 3.1 %all-to-all-done.1 = bf16[64,16,256]{2,1,0:T(8,128)(2,1)S(1)} async-done(((bf16[64,16,256]{2,1,0:T(8,128)(2,1)}), bf16[64,16,256]{2,1,0:T(8,128)(2,1)S(1)}, u32[]{:S(2)}, u32[]{:S(2)}) %all-to-all-start.1) | async-done | bytes 524320 | tf_op jit(solution)/shard_map/all_to_all | solution.py:43
  104.0 1.9 %collective-permute-start.7 = (bf16[16,1024]{1,0:T(8,128)(2,1)S(1)}, bf16[16,1024]{1,0:T(8,128)(2,1)S(1)}, u32[]{:S(2)}, u32[]{:S(2)}) collective-permute-start(bf16[16,1024]{1,0:T(8,128)(2,1)S(1)} %get-tuple-element.56), channel_id=1, source_target_pairs={{0,4},{1,5},{2,0},{3,1},{4,2},{5,3},{6,10},{7,11},{8,6},{9,7},{10,... | collective-permute-start | bytes 98312 | tf_op jit(solution)/shard_map/ppermute | solution.py:20
  105.9 3.4 %collective-permute-start.6 = (bf16[16,1024]{1,0:T(8,128)(2,1)S(1)}, bf16[16,1024]{1,0:T(8,128)(2,1)S(1)}, u32[]{:S(2)}, u32[]{:S(2)}) collective-permute-start(bf16[16,1024]{1,0:T(8,128)(2,1)S(1)} %get-tuple-element.56), channel_id=1, source_target_pairs={{0,2},{1,3},{2,4},{3,5},{4,0},{5,1},{6,8},{7,9},{8,10},{9,11},{10,... | collective-permute-start | bytes 98312 | tf_op jit(solution)/shard_map/ppermute | solution.py:20
  109.3 2.2 %collective-permute-done.6 = bf16[16,1024]{1,0:T(8,128)(2,1)S(1)} collective-permute-done((bf16[16,1024]{1,0:T(8,128)(2,1)S(1)}, bf16[16,1024]{1,0:T(8,128)(2,1)S(1)}, u32[]{:S(2)}, u32[]{:S(2)}) %collective-permute-start.6) | collective-permute-done | bytes 32800 | tf_op jit(solution)/shard_map/ppermute | solution.py:20
  111.5 3.9 %collective-permute-start.8 = (bf16[16,1024]{1,0:T(8,128)(2,1)S(1)}, bf16[16,1024]{1,0:T(8,128)(2,1)S(1)}, u32[]{:S(2)}, u32[]{:S(2)}) collective-permute-start(bf16[16,1024]{1,0:T(8,128)(2,1)S(1)} %fusion), channel_id=1, source_target_pairs={{0,6},{1,7},{2,8},{3,9},{4,10},{5,11},{6,0},{7,1},{8,2},{9,3},{10,... | collective-permute-start | bytes 98312 | tf_op jit(solution)/shard_map/ppermute | solution.py:20
  115.4 2.6 %collective-permute-done.8 = bf16[16,1024]{1,0:T(8,128)(2,1)S(1)} collective-permute-done((bf16[16,1024]{1,0:T(8,128)(2,1)S(1)}, bf16[16,1024]{1,0:T(8,128)(2,1)S(1)}, u32[]{:S(2)}, u32[]{:S(2)}) %collective-permute-start.8) | collective-permute-done | bytes 32800 | tf_op jit(solution)/shard_map/ppermute | solution.py:20
  118.0 5.2 %collective-permute-start.9 = (bf16[16,1024]{1,0:T(8,128)(2,1)S(1)}, bf16[16,1024]{1,0:T(8,128)(2,1)S(1)}, u32[]{:S(2)}, u32[]{:S(2)}) collective-permute-start(bf16[16,1024]{1,0:T(8,128)(2,1)S(1)} %add_convert_fusion.own), channel_id=1, source_target_pairs={{0,1},{1,0},{2,3},{3,2},{4,5},{5,4},{6,7},{7,6},{8,9},{9,8},{10,11... | collective-permute-start | bytes 98312 | tf_op jit(solution)/shard_map/ppermute | solution.py:20
  123.2 0.8 collective-permute-done.9.other
  (23 shorter events, 1.9 us)
Async XLA Ops:
  3.0 48.6 %collective-permute-start = (bf16[32,2,2048]{2,1,0:T(2,128)(2,1)}, bf16[32,2,2048]{2,1,0:T(2,128)(2,1)}, u32[]{:S(2)}, u32[]{:S(2)}) collective-permute-start(bf16[32,2,2048]{2,1,0:T(2,128)(2,1)} %dynamic-slice_bitcast_fusion), channel_id=1, source_target_pairs={{0,22},{1,23},{2,20},{3,21},{4,18},{5,19},{6,16},{7,17},{8,14},{9,... | collective-permute-start | bytes 786440 | tf_op jit(solution)/shard_map/ppermute | solution.py:36
  21.4 46.5 %all-to-all-start = ((bf16[64,24,256]{2,1,0:T(8,128)(2,1)}), bf16[64,24,256]{2,1,0:T(8,128)(2,1)S(1)}, u32[]{:S(2)}, u32[]{:S(2)}) async-start(bf16[64,24,256]{2,1,0:T(8,128)(2,1)} %bitcast.22), calls=%async_computation | async-start | bytes 1572864 | tf_op jit(solution)/shard_map/all_to_all | solution.py:43
  31.0 6.0 %copy-start.1 = (bf16[1,2,64,2,2048]{4,3,2,1,0:T(2,128)(2,1)S(1)}, bf16[1,2,64,2,2048]{4,3,2,1,0:T(2,128)(2,1)}, u32[]{:S(2)}) copy-start(bf16[1,2,64,2,2048]{4,3,2,1,0:T(2,128)(2,1)} %param.13) | copy-start | bytes 3145732
  33.8 17.8 %collective-permute-start.1 = (bf16[6144,128]{1,0:T(8,128)(2,1)}, bf16[6144,128]{1,0:T(8,128)(2,1)S(1)}, u32[]{:S(2)}, u32[]{:S(2)}) collective-permute-start(bf16[6144,128]{1,0:T(8,128)(2,1)} %shard_map.114), channel_id=1, source_target_pairs={{0,1},{1,0},{2,3},{3,2},{4,5},{5,4},{6,7},{7,6},{8,9},{9,8},{10,11... | collective-permute-start | bytes 4718600 | tf_op jit(solution)/shard_map/ppermute | solution.py:20
  41.6 10.0 %collective-permute-start.2 = (f32[512,128]{1,0:T(8,128)}, f32[512,128]{1,0:T(8,128)S(1)}, u32[]{:S(2)}, u32[]{:S(2)}) collective-permute-start(f32[512,128]{1,0:T(8,128)} %get-tuple-element.43.acts_in), channel_id=1, source_target_pairs={{0,1},{1,0},{2,3},{3,2},{4,5},{5,4},{6,7},{7,6},{8,9},{9,8},{10,11... | collective-permute-start | bytes 786440 | tf_op jit(solution)/shard_map/ppermute | solution.py:20
  51.6 24.1 %copy-start.6 = (f32[512,128]{1,0:T(8,128)}, f32[512,128]{1,0:T(8,128)S(1)}, u32[]{:S(2)}) copy-start(f32[512,128]{1,0:T(8,128)S(1)} %collective-permute-done.2.acts_got) | copy-start | bytes 786436
  51.6 16.3 %copy-start.2 = (bf16[6144,128]{1,0:T(8,128)(2,1)}, bf16[6144,128]{1,0:T(8,128)(2,1)S(1)}, u32[]{:S(2)}) copy-start(bf16[6144,128]{1,0:T(8,128)(2,1)S(1)} %collective-permute-done.1.packed) | copy-start | bytes 4718596
  67.9 0.9 copy-start.4
  71.5 15.6 %copy-start.5 = (bf16[64,24,256]{2,1,0:T(8,128)(2,1)S(1)}, bf16[64,24,256]{2,1,0:T(8,128)(2,1)}, u32[]{:S(2)}) copy-start(bf16[64,24,256]{2,1,0:T(8,128)(2,1)} %copy-done.4) | copy-start | bytes 2359300
  71.5 4.2 %collective-permute-start.3 = (f32[256,256]{1,0:T(8,128)}, f32[256,256]{1,0:T(8,128)S(1)}, u32[]{:S(2)}, u32[]{:S(2)}) collective-permute-start(f32[256,256]{1,0:T(8,128)} %get-tuple-element.42.part_in), channel_id=1, source_target_pairs={{0,1},{1,0},{2,3},{3,2},{4,5},{5,4},{6,7},{7,6},{8,9},{9,8},{10,11... | collective-permute-start | bytes 786440 | tf_op jit(solution)/shard_map/ppermute | solution.py:20
  75.7 0.7 copy-start.7
  80.0 23.5 %all-to-all-start.1 = ((bf16[64,16,256]{2,1,0:T(8,128)(2,1)}), bf16[64,16,256]{2,1,0:T(8,128)(2,1)S(1)}, u32[]{:S(2)}, u32[]{:S(2)}) async-start(bf16[64,16,256]{2,1,0:T(8,128)(2,1)} %bitcast.30), calls=%async_computation.1 | async-start | bytes 1048576 | tf_op jit(solution)/shard_map/all_to_all | solution.py:43
  87.1 7.1 %collective-permute-start.5 = (bf16[1536,256]{1,0:T(8,128)(2,1)S(1)}, bf16[1536,256]{1,0:T(8,128)(2,1)S(1)}, u32[]{:S(2)}, u32[]{:S(2)}) collective-permute-start(bf16[1536,256]{1,0:T(8,128)(2,1)S(1)} %bitcast.27), channel_id=1, source_target_pairs={{0,1},{1,0},{2,3},{3,2},{4,5},{5,4},{6,7},{7,6},{8,9},{9,8},{10,11... | collective-permute-start | bytes 2359304 | tf_op jit(solution)/shard_map/ppermute | solution.py:20
  89.7 3.7 %collective-permute-start.4 = (bf16[32,2,2048]{2,1,0:T(2,128)(2,1)}, bf16[32,2,2048]{2,1,0:T(2,128)(2,1)S(1)}, u32[]{:S(2)}, u32[]{:S(2)}) collective-permute-start(bf16[32,2,2048]{2,1,0:T(2,128)(2,1)} %collective-permute-done), channel_id=1, source_target_pairs={{0,1},{1,0},{2,3},{3,2},{4,5},{5,4},{6,7},{7,6},{8,9},{9,8},{10,11... | collective-permute-start | bytes 786440 | tf_op jit(solution)/shard_map/ppermute | solution.py:20
  94.2 0.9 copy-start.3
  95.1 8.5 %copy-start = (bf16[256,16]{1,0:T(8,128)(2,1)S(1)}, bf16[256,16]{1,0:T(8,128)(2,1)}, u32[]{:S(2)}) copy-start(bf16[256,16]{1,0:T(8,128)(2,1)} %get-tuple-element.54.place) | copy-start | bytes 24580
  104.0 5.3 %collective-permute-start.7 = (bf16[16,1024]{1,0:T(8,128)(2,1)S(1)}, bf16[16,1024]{1,0:T(8,128)(2,1)S(1)}, u32[]{:S(2)}, u32[]{:S(2)}) collective-permute-start(bf16[16,1024]{1,0:T(8,128)(2,1)S(1)} %get-tuple-element.56), channel_id=1, source_target_pairs={{0,4},{1,5},{2,0},{3,1},{4,2},{5,3},{6,10},{7,11},{8,6},{9,7},{10,... | collective-permute-start | bytes 98312 | tf_op jit(solution)/shard_map/ppermute | solution.py:20
  105.9 5.6 %collective-permute-start.6 = (bf16[16,1024]{1,0:T(8,128)(2,1)S(1)}, bf16[16,1024]{1,0:T(8,128)(2,1)S(1)}, u32[]{:S(2)}, u32[]{:S(2)}) collective-permute-start(bf16[16,1024]{1,0:T(8,128)(2,1)S(1)} %get-tuple-element.56), channel_id=1, source_target_pairs={{0,2},{1,3},{2,4},{3,5},{4,0},{5,1},{6,8},{7,9},{8,10},{9,11},{10,... | collective-permute-start | bytes 98312 | tf_op jit(solution)/shard_map/ppermute | solution.py:20
  111.5 6.5 %collective-permute-start.8 = (bf16[16,1024]{1,0:T(8,128)(2,1)S(1)}, bf16[16,1024]{1,0:T(8,128)(2,1)S(1)}, u32[]{:S(2)}, u32[]{:S(2)}) collective-permute-start(bf16[16,1024]{1,0:T(8,128)(2,1)S(1)} %fusion), channel_id=1, source_target_pairs={{0,6},{1,7},{2,8},{3,9},{4,10},{5,11},{6,0},{7,1},{8,2},{9,3},{10,... | collective-permute-start | bytes 98312 | tf_op jit(solution)/shard_map/ppermute | solution.py:20
  118.0 6.0 %collective-permute-start.9 = (bf16[16,1024]{1,0:T(8,128)(2,1)S(1)}, bf16[16,1024]{1,0:T(8,128)(2,1)S(1)}, u32[]{:S(2)}, u32[]{:S(2)}) collective-permute-start(bf16[16,1024]{1,0:T(8,128)(2,1)S(1)} %add_convert_fusion.own), channel_id=1, source_target_pairs={{0,1},{1,0},{2,3},{3,2},{4,5},{5,4},{6,7},{7,6},{8,9},{9,8},{10,11... | collective-permute-start | bytes 98312 | tf_op jit(solution)/shard_map/ppermute | solution.py:20

commit v4 on v3

--- a/solution.py
+++ b/solution.py
@@ -12,6 +12,7 @@
 GROUPS = 8
 VMEM = pl.BlockSpec(memory_space=pltpu.VMEM)
 ANY = pl.BlockSpec(memory_space=pl.ANY)
+HBM = pl.BlockSpec(memory_space=pltpu.HBM)
 SMEM = pl.BlockSpec(memory_space=pltpu.SMEM)
 
 
@@ -105,6 +106,13 @@
         rows[p][16 * g : 16 * g + 16, 256 * f : 256 * f + 256] for p in range(2) for f in range(4)
     ]
     return jnp.concatenate(parts)
+
+
+def part_kernel(saved, part, sem):
+    first = 32 * (lax.axis_index("dp") % 2)
+    copy = pltpu.make_async_copy(saved.at[0, 1, pl.ds(first, 32)], part, sem)
+    copy.start()
+    copy.wait()
 
 
 def prep_kernel(routes, probs, out_grad, outgoing_out, outgoing, sems):
@@ -381,8 +389,14 @@
     home_gu, home_d = home_gate_up[0], home_down[0]
     spare_gu, spare_d = replica_gate_up[0], replica_down[0]
 
-    core = lax.axis_index("dp") % 2
-    x_part = lax.dynamic_slice_in_dim(saved_inputs[0, 1], core * 32, 32, 0)
+    x_part = call(
+        part_kernel,
+        shape((32, 2, 2048)),
+        10**3,
+        10**5,
+        [ANY],
+        [pltpu.SemaphoreType.DMA(())],
+    )(saved_inputs)
     x_part, routes, route_probs = lax.optimization_barrier((x_part, routes, route_probs))
     x_part = to_next(x_part)
 
@@ -438,10 +452,11 @@
             pltpu.SemaphoreType.DMA((2,)),
         ],
         (ANY, ANY),
+        vmem=50,
     )(incoming, home_d, spare_d, packed)
     pair, grads = call(
         rows_kernel,
-        (shape((1024, 256)), shape((256, 256))),
+        (pltpu.HBM((1024, 256), BF), pltpu.HBM((256, 256), BF)),
         10**9,
         4 * 10**6,
         [ANY] * 7,
@@ -455,7 +470,8 @@
             pltpu.SemaphoreType.DMA((12,)),
             pltpu.SemaphoreType.DMA((3,)),
         ],
-        (ANY, ANY),
+        (HBM, HBM),
+        vmem=50,
     )(part, swap_cores(part), acts, acts_got, home_gu, spare_gu, packed)
     returned = exchange(pair)
 

time: 125 us -> 122 us (0.976)
  local copies, waits for them, and re-layouts: 8.59 us -> 4.7 us
    slice x1 -> x0, local copies, waits for them, and re-layouts: 1.41 us -> none  [on_device(): x_part = lax.dynamic_slice_in_dim(saved_inputs[0, 1], core * 32, 32, 0)]
    pallas_call x1 -> x2, Pallas kernels: 3.57 us -> 4.89 us  [the longest x1 3.21 us: on_device(): call(rows_kernel, (pltpu.HBM((1024, 256), BF), pltpu.HBM((256, 256), BF))...]
  transfers between devices with their start and end apart: 12 -> 12, of which waited for: 7 -> 8; matrix products, arithmetic and copies ran while one was open for 3% -> 2% of each run, Pallas kernels for 11% -> 12%
where the time goes in v4:
time: 122 us
  starting transfers between devices  59.2 us (49%)
  waiting for transfers between devices  35 us (29%)
  Pallas kernels  22 us (18%)
  local copies, waits for them, and re-layouts  4.7 us (4%)
    ppermute x9, starting transfers between devices, along_dp(): return lax.ppermute(array, 'dp', pairs)  26.7 us
    all_to_all x2, waiting for transfers between devices, exchange(): lax.all_to_all(array, ('ep', 'dp'), split_axis=0, concat_axis=0, axis_ind...  19.5 us
    all_to_all x2, starting transfers between devices, exchange(): lax.all_to_all(array, ('ep', 'dp'), split_axis=0, concat_axis=0, axis_ind...  17.4 us
    ppermute x1, starting transfers between devices, to_next(): return lax.ppermute(array, ('ep', 'dp'), pairs)  15.1 us
    ppermute x1, waiting for transfers between devices, to_next(): return lax.ppermute(array, ('ep', 'dp'), pairs)  8.02 us
    ppermute x9, waiting for transfers between devices, along_dp(): return lax.ppermute(array, 'dp', pairs)  7.41 us
    pallas_call x1, Pallas kernels, on_device(): call(weights_kernel, (shape((2, 2048, 128)), shape((128, 2048))), 10 ** 8...  5.37 us
    pallas_call x1, Pallas kernels, on_device(): call(act_kernel, (shape((512, 128), F32), shape((256, 128)), shape((256,...  3.41 us
  transfers between devices with their start and end apart: 12, of which 8 were waited for; matrix products, arithmetic and copies ran while one was open for 2% of the time, Pallas kernels for 12%

profile of v4, /device:TPU:1, one launch (start us, length us, event | category | flops | bytes accessed | tf_op | source)
XLA Modules:
  0.0 121.7 jit_solution(3370280234897176975)
XLA Ops:
  0.6 1.7 %shard_map.112 = bf16[32,2,2048]{2,1,0:T(2,128)(2,1)} custom-call(bf16[1,2,64,2,2048]{4,3,2,1,0:T(2,128)(2,1)} %saved.1), custom_call_target="tpu_custom_call" | custom-call | flops 1000 | bytes 100000 | tf_op jit(solution)/shard_map/pallas_call | solution.py:392
  2.3 15.1 %collective-permute-start = (bf16[32,2,2048]{2,1,0:T(2,128)(2,1)}, bf16[32,2,2048]{2,1,0:T(2,128)(2,1)S(1)}, u32[]{:S(2)}, u32[]{:S(2)}) collective-permute-start(bf16[32,2,2048]{2,1,0:T(2,128)(2,1)} %shard_map.112), channel_id=1, source_target_pairs={{0,22},{1,23},{2,20},{3,21},{4,18},{5,19},{6,16},{7,17},{8,14},{9,... | collective-permute-start | bytes 786440 | tf_op jit(solution)/shard_map/ppermute | solution.py:37
  17.5 2.6 %shard_map.113 = bf16[1536,256]{1,0:T(8,128)(2,1)} custom-call(s32[8,16]{1,0:T(8,128)} %bitcast.30, f32[8,16]{1,0:T(8,128)} %bitcast.29, bf16[16,2048]{1,0:T(8,128)(2,1)} %out_grad.1), custom_call_target="tpu_custom_call" | custom-call | flops 1000000 | bytes 1000000 | tf_op jit(solution)/shard_map/pallas_call | solution.py:403
  20.1 10.3 %all-to-all-start = ((bf16[64,24,256]{2,1,0:T(8,128)(2,1)}), bf16[64,24,256]{2,1,0:T(8,128)(2,1)S(1)}, u32[]{:S(2)}, u32[]{:S(2)}) async-start(bf16[64,24,256]{2,1,0:T(8,128)(2,1)} %bitcast.27), calls=%async_computation | async-start | bytes 1572864 | tf_op jit(solution)/shard_map/all_to_all | solution.py:44
  30.4 2.8 %shard_map.115 = bf16[6144,128]{1,0:T(8,128)(2,1)} custom-call(bf16[128,2048]{1,0:T(8,128)(2,1)} %bitcast.19, bf16[128,2048]{1,0:T(8,128)(2,1)} %bitcast.25, bf16[2,2048,128]{2,1,0:T(8,128)(2,1)} %bitcast.12, bf16[2,2048,128]{2,1,0:T(8,128)(2,1)} %bitcast.16), custom_call_target="tpu_custom_call" | custom-call | flops 1000000 | bytes 1000000 | tf_op jit(solution)/shard_map/pallas_call | solution.py:424
  33.2 3.1 %collective-permute-start.1 = (bf16[6144,128]{1,0:T(8,128)(2,1)}, bf16[6144,128]{1,0:T(8,128)(2,1)}, u32[]{:S(2)}, u32[]{:S(2)}) collective-permute-start(bf16[6144,128]{1,0:T(8,128)(2,1)} %shard_map.115), channel_id=1, source_target_pairs={{0,1},{1,0},{2,3},{3,2},{4,5},{5,4},{6,7},{7,6},{8,9},{9,8},{10,11... | collective-permute-start | bytes 4718600 | tf_op jit(solution)/shard_map/ppermute | solution.py:21
  36.4 1.2 %reshape.29.x = bf16[256,2048]{1,0:T(8,128)(2,1)} reshape(bf16[1,2,64,2,2048]{4,3,2,1,0:T(2,128)(2,1)S(1)} %copy-done.7) | data formatting | bytes 2097152 | tf_op jit(solution)/shard_map/reshape | solution.py:415
  37.6 3.4 %shard_map.114 = (f32[512,128]{1,0:T(8,128)}, bf16[256,128]{1,0:T(8,128)(2,1)}, bf16[256,16]{1,0:T(8,128)(2,1)}) custom-call(bf16[256,2048]{1,0:T(8,128)(2,1)} %reshape.29.x, bf16[2,2048,128]{2,1,0:T(8,128)(2,1)} %bitcast.13, bf16[2,2048,128]{2,1,0:T(8,128)(2,1)} %bitcast.17, s32[8,16]{1,0:T(8,128)} %bitcast.31), custom_call_target="tpu_custom_call" | custom-call | flops 99999997952 | bytes 4000000 | tf_op jit(solution)/shard_map/pallas_call | solution.py:416
  41.0 1.9 %collective-permute-start.2 = (f32[512,128]{1,0:T(8,128)}, f32[512,128]{1,0:T(8,128)S(1)}, u32[]{:S(2)}, u32[]{:S(2)}) collective-permute-start(f32[512,128]{1,0:T(8,128)} %get-tuple-element.43.acts_in), channel_id=1, source_target_pairs={{0,1},{1,0},{2,3},{3,2},{4,5},{5,4},{6,7},{7,6},{8,9},{9,8},{10,11... | collective-permute-start | bytes 786440 | tf_op jit(solution)/shard_map/ppermute | solution.py:21
  42.9 8.0 %collective-permute-done = bf16[32,2,2048]{2,1,0:T(2,128)(2,1)S(1)} collective-permute-done((bf16[32,2,2048]{2,1,0:T(2,128)(2,1)}, bf16[32,2,2048]{2,1,0:T(2,128)(2,1)S(1)}, u32[]{:S(2)}, u32[]{:S(2)}) %collective-permute-start) | collective-permute-done | bytes 262176 | tf_op jit(solution)/shard_map/ppermute | solution.py:37
  51.0 16.3 %all-to-all-done = bf16[64,24,256]{2,1,0:T(8,128)(2,1)S(1)} async-done(((bf16[64,24,256]{2,1,0:T(8,128)(2,1)}), bf16[64,24,256]{2,1,0:T(8,128)(2,1)S(1)}, u32[]{:S(2)}, u32[]{:S(2)}) %all-to-all-start) | async-done | bytes 786464 | tf_op jit(solution)/shard_map/all_to_all | solution.py:44
  67.3 1.8 %shard_map.116 = (f32[256,256]{1,0:T(8,128)S(1)}, bf16[384,1024]{1,0:T(8,128)(2,1)S(1)}) custom-call(bf16[1536,256]{1,0:T(8,128)(2,1)S(1)} %bitcast.23, bf16[128,2048]{1,0:T(8,128)(2,1)S(1)} %bitcast.21, bf16[128,2048]{1,0:T(8,128)(2,1)S(1)} %bitcast.26, bf16[6144,128]{1,0:T(8,128)(2,1)} %collective-permute-done.1.packed), custom_call_target="tpu_custom_call" | custom-call | flops 1000000000 | bytes 4000000 | tf_op jit(solution)/shard_map/pallas_call | solution.py:439
  69.1 0.9 copy-done.3
  70.0 2.7 %collective-permute-start.3 = (f32[256,256]{1,0:T(8,128)S(1)}, f32[256,256]{1,0:T(8,128)S(1)}, u32[]{:S(2)}, u32[]{:S(2)}) collective-permute-start(f32[256,256]{1,0:T(8,128)S(1)} %get-tuple-element.42.part_in), channel_id=1, source_target_pairs={{0,1},{1,0},{2,3},{3,2},{4,5},{5,4},{6,7},{7,6},{8,9},{9,8},{10,11... | collective-permute-start | bytes 786440 | tf_op jit(solution)/shard_map/ppermute | solution.py:21
  72.7 1.1 collective-permute-done.3.part_got
  73.8 3.2 %shard_map.117 = (bf16[1024,256]{1,0:T(8,128)(2,1)}, bf16[256,256]{1,0:T(8,128)(2,1)}) custom-call(f32[256,256]{1,0:T(8,128)S(1)} %get-tuple-element.42.part_in, f32[256,256]{1,0:T(8,128)S(1)} %collective-permute-done.3.part_got, f32[512,128]{1,0:T(8,128)S(1)} %copy-done.5, f32[512,128]{1,0:T(8,128)S(1)} %collective-permute-done.2.acts_got, ...), custom_call_target="tpu_custom_call" | custom-call | flops 1000000000 | bytes 4000000 | tf_op jit(solution)/shard_map/pallas_call | solution.py:457
  77.0 7.1 %all-to-all-start.1 = ((bf16[64,16,256]{2,1,0:T(8,128)(2,1)}), bf16[64,16,256]{2,1,0:T(8,128)(2,1)S(1)}, u32[]{:S(2)}, u32[]{:S(2)}) async-start(bf16[64,16,256]{2,1,0:T(8,128)(2,1)} %bitcast.28), calls=%async_computation.1 | async-start | bytes 1048576 | tf_op jit(solution)/shard_map/all_to_all | solution.py:44
  84.2 2.6 %collective-permute-start.5 = (bf16[1536,256]{1,0:T(8,128)(2,1)S(1)}, bf16[1536,256]{1,0:T(8,128)(2,1)S(1)}, u32[]{:S(2)}, u32[]{:S(2)}) collective-permute-start(bf16[1536,256]{1,0:T(8,128)(2,1)S(1)} %bitcast.24), channel_id=1, source_target_pairs={{0,1},{1,0},{2,3},{3,2},{4,5},{5,4},{6,7},{7,6},{8,9},{9,8},{10,11... | collective-permute-start | bytes 2359304 | tf_op jit(solution)/shard_map/ppermute | solution.py:21
  86.8 1.9 %collective-permute-start.4 = (bf16[32,2,2048]{2,1,0:T(2,128)(2,1)S(1)}, bf16[32,2,2048]{2,1,0:T(2,128)(2,1)S(1)}, u32[]{:S(2)}, u32[]{:S(2)}) collective-permute-start(bf16[32,2,2048]{2,1,0:T(2,128)(2,1)S(1)} %collective-permute-done), channel_id=1, source_target_pairs={{0,1},{1,0},{2,3},{3,2},{4,5},{5,4},{6,7},{7,6},{8,9},{9,8},{10,11... | collective-permute-start | bytes 786440 | tf_op jit(solution)/shard_map/ppermute | solution.py:21
  88.7 0.8 reshape.32.x_own
  89.5 0.7 collective-permute-done.4
  90.2 0.8 reshape.33.x_other
  91.0 0.9 copy-done.8
  91.9 5.4 %shard_map.118 = (bf16[2,2048,128]{2,1,0:T(8,128)(2,1)}, bf16[128,2048]{1,0:T(8,128)(2,1)}) custom-call(s32[64]{0:T(128)} %experts.1, bf16[256,2048]{1,0:T(8,128)(2,1)} %reshape.29.x, bf16[64,2048]{1,0:T(8,128)(2,1)} %reshape.32.x_own, bf16[64,2048]{1,0:T(8,128)(2,1)} %reshape.33.x_other, bf16[384,1024]{1,0:T(8,128)(2,1)} %copy-done.3, ...), custom_call_target="tpu_custom_call" | custom-call | flops 100000000 | bytes 1000000 | tf_op jit(solution)/shard_map/pallas_call | solution.py:479
  97.3 3.3 %all-to-all-done.1 = bf16[64,16,256]{2,1,0:T(8,128)(2,1)S(1)} async-done(((bf16[64,16,256]{2,1,0:T(8,128)(2,1)}), bf16[64,16,256]{2,1,0:T(8,128)(2,1)S(1)}, u32[]{:S(2)}, u32[]{:S(2)}) %all-to-all-start.1) | async-done | bytes 524320 | tf_op jit(solution)/shard_map/all_to_all | solution.py:44
  101.0 1.9 %collective-permute-start.7 = (bf16[16,1024]{1,0:T(8,128)(2,1)S(1)}, bf16[16,1024]{1,0:T(8,128)(2,1)S(1)}, u32[]{:S(2)}, u32[]{:S(2)}) collective-permute-start(bf16[16,1024]{1,0:T(8,128)(2,1)S(1)} %get-tuple-element.56), channel_id=1, source_target_pairs={{0,4},{1,5},{2,0},{3,1},{4,2},{5,3},{6,10},{7,11},{8,6},{9,7},{10,... | collective-permute-start | bytes 98312 | tf_op jit(solution)/shard_map/ppermute | solution.py:21
  103.0 3.4 %collective-permute-start.6 = (bf16[16,1024]{1,0:T(8,128)(2,1)S(1)}, bf16[16,1024]{1,0:T(8,128)(2,1)S(1)}, u32[]{:S(2)}, u32[]{:S(2)}) collective-permute-start(bf16[16,1024]{1,0:T(8,128)(2,1)S(1)} %get-tuple-element.56), channel_id=1, source_target_pairs={{0,2},{1,3},{2,4},{3,5},{4,0},{5,1},{6,8},{7,9},{8,10},{9,11},{10,... | collective-permute-start | bytes 98312 | tf_op jit(solution)/shard_map/ppermute | solution.py:21
  106.3 2.2 %collective-permute-done.6 = bf16[16,1024]{1,0:T(8,128)(2,1)S(1)} collective-permute-done((bf16[16,1024]{1,0:T(8,128)(2,1)S(1)}, bf16[16,1024]{1,0:T(8,128)(2,1)S(1)}, u32[]{:S(2)}, u32[]{:S(2)}) %collective-permute-start.6) | collective-permute-done | bytes 32800 | tf_op jit(solution)/shard_map/ppermute | solution.py:21
  108.5 3.9 %collective-permute-start.8 = (bf16[16,1024]{1,0:T(8,128)(2,1)S(1)}, bf16[16,1024]{1,0:T(8,128)(2,1)S(1)}, u32[]{:S(2)}, u32[]{:S(2)}) collective-permute-start(bf16[16,1024]{1,0:T(8,128)(2,1)S(1)} %fusion), channel_id=1, source_target_pairs={{0,6},{1,7},{2,8},{3,9},{4,10},{5,11},{6,0},{7,1},{8,2},{9,3},{10,... | collective-permute-start | bytes 98312 | tf_op jit(solution)/shard_map/ppermute | solution.py:21
  112.4 2.6 %collective-permute-done.8 = bf16[16,1024]{1,0:T(8,128)(2,1)S(1)} collective-permute-done((bf16[16,1024]{1,0:T(8,128)(2,1)S(1)}, bf16[16,1024]{1,0:T(8,128)(2,1)S(1)}, u32[]{:S(2)}, u32[]{:S(2)}) %collective-permute-start.8) | collective-permute-done | bytes 32800 | tf_op jit(solution)/shard_map/ppermute | solution.py:21
  115.0 5.3 %collective-permute-start.9 = (bf16[16,1024]{1,0:T(8,128)(2,1)S(1)}, bf16[16,1024]{1,0:T(8,128)(2,1)S(1)}, u32[]{:S(2)}, u32[]{:S(2)}) collective-permute-start(bf16[16,1024]{1,0:T(8,128)(2,1)S(1)} %add_convert_fusion.own), channel_id=1, source_target_pairs={{0,1},{1,0},{2,3},{3,2},{4,5},{5,4},{6,7},{7,6},{8,9},{9,8},{10,11... | collective-permute-start | bytes 98312 | tf_op jit(solution)/shard_map/ppermute | solution.py:21
  120.3 0.8 collective-permute-done.9.other
  (24 shorter events, 1.2 us)
Async XLA Ops:
  2.3 48.6 %collective-permute-start = (bf16[32,2,2048]{2,1,0:T(2,128)(2,1)}, bf16[32,2,2048]{2,1,0:T(2,128)(2,1)S(1)}, u32[]{:S(2)}, u32[]{:S(2)}) collective-permute-start(bf16[32,2,2048]{2,1,0:T(2,128)(2,1)} %shard_map.112), channel_id=1, source_target_pairs={{0,22},{1,23},{2,20},{3,21},{4,18},{5,19},{6,16},{7,17},{8,14},{9,... | collective-permute-start | bytes 786440 | tf_op jit(solution)/shard_map/ppermute | solution.py:37
  20.1 47.1 %all-to-all-start = ((bf16[64,24,256]{2,1,0:T(8,128)(2,1)}), bf16[64,24,256]{2,1,0:T(8,128)(2,1)S(1)}, u32[]{:S(2)}, u32[]{:S(2)}) async-start(bf16[64,24,256]{2,1,0:T(8,128)(2,1)} %bitcast.27), calls=%async_computation | async-start | bytes 1572864 | tf_op jit(solution)/shard_map/all_to_all | solution.py:44
  30.4 6.0 %copy-start.7 = (bf16[1,2,64,2,2048]{4,3,2,1,0:T(2,128)(2,1)S(1)}, bf16[1,2,64,2,2048]{4,3,2,1,0:T(2,128)(2,1)}, u32[]{:S(2)}) copy-start(bf16[1,2,64,2,2048]{4,3,2,1,0:T(2,128)(2,1)} %saved.1) | copy-start | bytes 3145732
  33.2 17.8 %collective-permute-start.1 = (bf16[6144,128]{1,0:T(8,128)(2,1)}, bf16[6144,128]{1,0:T(8,128)(2,1)}, u32[]{:S(2)}, u32[]{:S(2)}) collective-permute-start(bf16[6144,128]{1,0:T(8,128)(2,1)} %shard_map.115), channel_id=1, source_target_pairs={{0,1},{1,0},{2,3},{3,2},{4,5},{5,4},{6,7},{7,6},{8,9},{9,8},{10,11... | collective-permute-start | bytes 4718600 | tf_op jit(solution)/shard_map/ppermute | solution.py:21
  37.6 29.6 %copy-start.2 = (bf16[1,128,2048]{2,1,0:T(8,128)(2,1)S(1)}, bf16[1,128,2048]{2,1,0:T(8,128)(2,1)}, u32[]{:S(2)}) copy-start(bf16[1,128,2048]{2,1,0:T(8,128)(2,1)} %param.15) | copy-start | bytes 1572868
  37.6 29.6 %copy-start.4 = (bf16[1,128,2048]{2,1,0:T(8,128)(2,1)S(1)}, bf16[1,128,2048]{2,1,0:T(8,128)(2,1)}, u32[]{:S(2)}) copy-start(bf16[1,128,2048]{2,1,0:T(8,128)(2,1)} %param.17) | copy-start | bytes 1572868
  41.0 9.9 %collective-permute-start.2 = (f32[512,128]{1,0:T(8,128)}, f32[512,128]{1,0:T(8,128)S(1)}, u32[]{:S(2)}, u32[]{:S(2)}) collective-permute-start(f32[512,128]{1,0:T(8,128)} %get-tuple-element.43.acts_in), channel_id=1, source_target_pairs={{0,1},{1,0},{2,3},{3,2},{4,5},{5,4},{6,7},{7,6},{8,9},{9,8},{10,11... | collective-permute-start | bytes 786440 | tf_op jit(solution)/shard_map/ppermute | solution.py:21
  67.2 6.6 %copy-start = (bf16[1,2,2048,128]{3,2,1,0:T(8,128)(2,1)S(1)}, bf16[1,2,2048,128]{3,2,1,0:T(8,128)(2,1)}, u32[]{:S(2)}) copy-start(bf16[1,2,2048,128]{3,2,1,0:T(8,128)(2,1)} %param.14) | copy-start | bytes 3145732
  67.2 6.6 %copy-start.1 = (bf16[1,2,2048,128]{3,2,1,0:T(8,128)(2,1)S(1)}, bf16[1,2,2048,128]{3,2,1,0:T(8,128)(2,1)}, u32[]{:S(2)}) copy-start(bf16[1,2,2048,128]{3,2,1,0:T(8,128)(2,1)} %param.16) | copy-start | bytes 3145732
  67.3 6.6 %copy-start.5 = (f32[512,128]{1,0:T(8,128)S(1)}, f32[512,128]{1,0:T(8,128)}, u32[]{:S(2)}) copy-start(f32[512,128]{1,0:T(8,128)} %get-tuple-element.43.acts_in) | copy-start | bytes 786436
  69.1 0.9 copy-start.3
  70.0 3.8 %collective-permute-start.3 = (f32[256,256]{1,0:T(8,128)S(1)}, f32[256,256]{1,0:T(8,128)S(1)}, u32[]{:S(2)}, u32[]{:S(2)}) collective-permute-start(f32[256,256]{1,0:T(8,128)S(1)} %get-tuple-element.42.part_in), channel_id=1, source_target_pairs={{0,1},{1,0},{2,3},{3,2},{4,5},{5,4},{6,7},{7,6},{8,9},{9,8},{10,11... | collective-permute-start | bytes 786440 | tf_op jit(solution)/shard_map/ppermute | solution.py:21
  77.0 23.5 %all-to-all-start.1 = ((bf16[64,16,256]{2,1,0:T(8,128)(2,1)}), bf16[64,16,256]{2,1,0:T(8,128)(2,1)S(1)}, u32[]{:S(2)}, u32[]{:S(2)}) async-start(bf16[64,16,256]{2,1,0:T(8,128)(2,1)} %bitcast.28), calls=%async_computation.1 | async-start | bytes 1048576 | tf_op jit(solution)/shard_map/all_to_all | solution.py:44
  84.2 6.8 %collective-permute-start.5 = (bf16[1536,256]{1,0:T(8,128)(2,1)S(1)}, bf16[1536,256]{1,0:T(8,128)(2,1)S(1)}, u32[]{:S(2)}, u32[]{:S(2)}) collective-permute-start(bf16[1536,256]{1,0:T(8,128)(2,1)S(1)} %bitcast.24), channel_id=1, source_target_pairs={{0,1},{1,0},{2,3},{3,2},{4,5},{5,4},{6,7},{7,6},{8,9},{9,8},{10,11... | collective-permute-start | bytes 2359304 | tf_op jit(solution)/shard_map/ppermute | solution.py:21
  86.8 3.4 %collective-permute-start.4 = (bf16[32,2,2048]{2,1,0:T(2,128)(2,1)S(1)}, bf16[32,2,2048]{2,1,0:T(2,128)(2,1)S(1)}, u32[]{:S(2)}, u32[]{:S(2)}) collective-permute-start(bf16[32,2,2048]{2,1,0:T(2,128)(2,1)S(1)} %collective-permute-done), channel_id=1, source_target_pairs={{0,1},{1,0},{2,3},{3,2},{4,5},{5,4},{6,7},{7,6},{8,9},{9,8},{10,11... | collective-permute-start | bytes 786440 | tf_op jit(solution)/shard_map/ppermute | solution.py:21
  91.0 0.9 copy-start.8
  91.9 8.6 %copy-start.6 = (bf16[256,16]{1,0:T(8,128)(2,1)S(1)}, bf16[256,16]{1,0:T(8,128)(2,1)}, u32[]{:S(2)}) copy-start(bf16[256,16]{1,0:T(8,128)(2,1)} %get-tuple-element.54.place) | copy-start | bytes 24580
  101.0 5.3 %collective-permute-start.7 = (bf16[16,1024]{1,0:T(8,128)(2,1)S(1)}, bf16[16,1024]{1,0:T(8,128)(2,1)S(1)}, u32[]{:S(2)}, u32[]{:S(2)}) collective-permute-start(bf16[16,1024]{1,0:T(8,128)(2,1)S(1)} %get-tuple-element.56), channel_id=1, source_target_pairs={{0,4},{1,5},{2,0},{3,1},{4,2},{5,3},{6,10},{7,11},{8,6},{9,7},{10,... | collective-permute-start | bytes 98312 | tf_op jit(solution)/shard_map/ppermute | solution.py:21
  103.0 5.6 %collective-permute-start.6 = (bf16[16,1024]{1,0:T(8,128)(2,1)S(1)}, bf16[16,1024]{1,0:T(8,128)(2,1)S(1)}, u32[]{:S(2)}, u32[]{:S(2)}) collective-permute-start(bf16[16,1024]{1,0:T(8,128)(2,1)S(1)} %get-tuple-element.56), channel_id=1, source_target_pairs={{0,2},{1,3},{2,4},{3,5},{4,0},{5,1},{6,8},{7,9},{8,10},{9,11},{10,... | collective-permute-start | bytes 98312 | tf_op jit(solution)/shard_map/ppermute | solution.py:21
  108.5 6.5 %collective-permute-start.8 = (bf16[16,1024]{1,0:T(8,128)(2,1)S(1)}, bf16[16,1024]{1,0:T(8,128)(2,1)S(1)}, u32[]{:S(2)}, u32[]{:S(2)}) collective-permute-start(bf16[16,1024]{1,0:T(8,128)(2,1)S(1)} %fusion), channel_id=1, source_target_pairs={{0,6},{1,7},{2,8},{3,9},{4,10},{5,11},{6,0},{7,1},{8,2},{9,3},{10,... | collective-permute-start | bytes 98312 | tf_op jit(solution)/shard_map/ppermute | solution.py:21
  115.0 6.1 %collective-permute-start.9 = (bf16[16,1024]{1,0:T(8,128)(2,1)S(1)}, bf16[16,1024]{1,0:T(8,128)(2,1)S(1)}, u32[]{:S(2)}, u32[]{:S(2)}) collective-permute-start(bf16[16,1024]{1,0:T(8,128)(2,1)S(1)} %add_convert_fusion.own), channel_id=1, source_target_pairs={{0,1},{1,0},{2,3},{3,2},{4,5},{5,4},{6,7},{7,6},{8,9},{9,8},{10,11... | collective-permute-start | bytes 98312 | tf_op jit(solution)/shard_map/ppermute | solution.py:21

commit v5 on v4

--- a/solution.py
+++ b/solution.py
@@ -483,6 +483,7 @@
         10**6,
         [SMEM] + [VMEM] * 9,
         [pltpu.VMEM((128, 2048), BF), pltpu.VMEM((384, 2048), BF)],
+        vmem=40,
     )(
         replica_expert,
         x,

time: 122 us -> 124 us (1.016)
  local copies, waits for them, and re-layouts: 4.7 us -> 8.73 us
  waiting for transfers between devices: 35 us -> 33.1 us
    unnamed x18 -> x30, local copies, waits for them, and re-layouts: 1.82 us -> 4.71 us
    all_to_all x2, waiting for transfers between devices: 19.5 us -> 17.5 us  [exchange(): lax.all_to_all(array, ('ep', 'dp'), split_axis=0, concat_axis=0, axis_ind...]
    pallas_call x1, Pallas kernels: 5.37 us -> 4.12 us  [on_device(): call(weights_kernel, (shape((2, 2048, 128)), shape((128, 2048))), 10 ** 8...]
  transfers between devices with their start and end apart: 12 -> 12, of which waited for: 8 -> 8; matrix products, arithmetic and copies ran while one was open for 2% -> 3% of each run, Pallas kernels for 12% -> 10%
where the time goes in v5:
time: 124 us; the launch traced here: 123 us
  starting transfers between devices  59.3 us (48%)
  waiting for transfers between devices  33.1 us (27%)
  Pallas kernels  20.9 us (17%)
  local copies, waits for them, and re-layouts  8.73 us (7%)
    ppermute x9, starting transfers between devices, along_dp(): return lax.ppermute(array, 'dp', pairs)  26.6 us
    all_to_all x2, waiting for transfers between devices, exchange(): lax.all_to_all(array, ('ep', 'dp'), split_axis=0, concat_axis=0, axis_ind...  17.5 us
    all_to_all x2, starting transfers between devices, exchange(): lax.all_to_all(array, ('ep', 'dp'), split_axis=0, concat_axis=0, axis_ind...  16.9 us
    ppermute x1, starting transfers between devices, to_next(): return lax.ppermute(array, ('ep', 'dp'), pairs)  15.8 us
    ppermute x1, waiting for transfers between devices, to_next(): return lax.ppermute(array, ('ep', 'dp'), pairs)  8.08 us
    ppermute x9, waiting for transfers between devices, along_dp(): return lax.ppermute(array, 'dp', pairs)  7.54 us
    unnamed x30, local copies, waits for them, and re-layouts  4.71 us
    pallas_call x1, Pallas kernels, on_device(): call(weights_kernel, (shape((2, 2048, 128)), shape((128, 2048))), 10 ** 8...  4.12 us
  transfers between devices with their start and end apart: 12, of which 8 were waited for; matrix products, arithmetic and copies ran while one was open for 3% of the time, Pallas kernels for 10%

profile of v5, /device:TPU:1, one launch (start us, length us, event | category | flops | bytes accessed | tf_op | source)
XLA Modules:
  0.0 123.0 jit_solution(13828658263483382678)
XLA Ops:
  0.6 1.7 %shard_map.112 = bf16[32,2,2048]{2,1,0:T(2,128)(2,1)} custom-call(bf16[1,2,64,2,2048]{4,3,2,1,0:T(2,128)(2,1)} %saved.1), custom_call_target="tpu_custom_call" | custom-call | flops 1000 | bytes 100000 | tf_op jit(solution)/shard_map/pallas_call | solution.py:392
  2.3 15.8 %collective-permute-start = (bf16[32,2,2048]{2,1,0:T(2,128)(2,1)}, bf16[32,2,2048]{2,1,0:T(2,128)(2,1)}, u32[]{:S(2)}, u32[]{:S(2)}) collective-permute-start(bf16[32,2,2048]{2,1,0:T(2,128)(2,1)} %shard_map.112), channel_id=1, source_target_pairs={{0,22},{1,23},{2,20},{3,21},{4,18},{5,19},{6,16},{7,17},{8,14},{9,... | collective-permute-start | bytes 786440 | tf_op jit(solution)/shard_map/ppermute | solution.py:37
  18.2 2.6 %shard_map.113 = bf16[1536,256]{1,0:T(8,128)(2,1)} custom-call(s32[8,16]{1,0:T(8,128)} %bitcast.30, f32[8,16]{1,0:T(8,128)} %bitcast.29, bf16[16,2048]{1,0:T(8,128)(2,1)} %out_grad.1), custom_call_target="tpu_custom_call" | custom-call | flops 1000000 | bytes 1000000 | tf_op jit(solution)/shard_map/pallas_call | solution.py:403
  20.8 9.6 %all-to-all-start = ((bf16[64,24,256]{2,1,0:T(8,128)(2,1)}), bf16[64,24,256]{2,1,0:T(8,128)(2,1)S(1)}, u32[]{:S(2)}, u32[]{:S(2)}) async-start(bf16[64,24,256]{2,1,0:T(8,128)(2,1)} %bitcast.27), calls=%async_computation | async-start | bytes 1572864 | tf_op jit(solution)/shard_map/all_to_all | solution.py:44
  30.4 2.7 %shard_map.115 = bf16[6144,128]{1,0:T(8,128)(2,1)} custom-call(bf16[128,2048]{1,0:T(8,128)(2,1)} %bitcast.19, bf16[128,2048]{1,0:T(8,128)(2,1)} %bitcast.25, bf16[2,2048,128]{2,1,0:T(8,128)(2,1)} %bitcast.12, bf16[2,2048,128]{2,1,0:T(8,128)(2,1)} %bitcast.16), custom_call_target="tpu_custom_call" | custom-call | flops 1000000 | bytes 1000000 | tf_op jit(solution)/shard_map/pallas_call | solution.py:424
  33.2 3.1 %collective-permute-start.1 = (bf16[6144,128]{1,0:T(8,128)(2,1)}, bf16[6144,128]{1,0:T(8,128)(2,1)}, u32[]{:S(2)}, u32[]{:S(2)}) collective-permute-start(bf16[6144,128]{1,0:T(8,128)(2,1)} %shard_map.115), channel_id=1, source_target_pairs={{0,1},{1,0},{2,3},{3,2},{4,5},{5,4},{6,7},{7,6},{8,9},{9,8},{10,11... | collective-permute-start | bytes 4718600 | tf_op jit(solution)/shard_map/ppermute | solution.py:21
  36.3 1.2 reshape.29.x
  37.6 3.4 %shard_map.114 = (f32[512,128]{1,0:T(8,128)}, bf16[256,128]{1,0:T(8,128)(2,1)}, bf16[256,16]{1,0:T(8,128)(2,1)}) custom-call(bf16[256,2048]{1,0:T(8,128)(2,1)} %reshape.29.x, bf16[2,2048,128]{2,1,0:T(8,128)(2,1)} %bitcast.13, bf16[2,2048,128]{2,1,0:T(8,128)(2,1)} %bitcast.17, s32[8,16]{1,0:T(8,128)} %bitcast.31), custom_call_target="tpu_custom_call" | custom-call | flops 99999997952 | bytes 4000000 | tf_op jit(solution)/shard_map/pallas_call | solution.py:416
  41.0 1.9 %collective-permute-start.2 = (f32[512,128]{1,0:T(8,128)}, f32[512,128]{1,0:T(8,128)S(1)}, u32[]{:S(2)}, u32[]{:S(2)}) collective-permute-start(f32[512,128]{1,0:T(8,128)} %get-tuple-element.43.acts_in), channel_id=1, source_target_pairs={{0,1},{1,0},{2,3},{3,2},{4,5},{5,4},{6,7},{7,6},{8,9},{9,8},{10,11... | collective-permute-start | bytes 786440 | tf_op jit(solution)/shard_map/ppermute | solution.py:21
  42.9 8.1 %collective-permute-done = bf16[32,2,2048]{2,1,0:T(2,128)(2,1)} collective-permute-done((bf16[32,2,2048]{2,1,0:T(2,128)(2,1)}, bf16[32,2,2048]{2,1,0:T(2,128)(2,1)}, u32[]{:S(2)}, u32[]{:S(2)}) %collective-permute-start) | collective-permute-done | bytes 262176 | tf_op jit(solution)/shard_map/ppermute | solution.py:37
  51.0 16.3 %all-to-all-done = bf16[64,24,256]{2,1,0:T(8,128)(2,1)S(1)} async-done(((bf16[64,24,256]{2,1,0:T(8,128)(2,1)}), bf16[64,24,256]{2,1,0:T(8,128)(2,1)S(1)}, u32[]{:S(2)}, u32[]{:S(2)}) %all-to-all-start) | async-done | bytes 786464 | tf_op jit(solution)/shard_map/all_to_all | solution.py:44
  67.3 2.0 %shard_map.116 = (f32[256,256]{1,0:T(8,128)S(1)}, bf16[384,1024]{1,0:T(8,128)(2,1)S(1)}) custom-call(bf16[1536,256]{1,0:T(8,128)(2,1)S(1)} %bitcast.23, bf16[128,2048]{1,0:T(8,128)(2,1)S(1)} %bitcast.20, bf16[128,2048]{1,0:T(8,128)(2,1)S(1)} %bitcast.26, bf16[6144,128]{1,0:T(8,128)(2,1)} %collective-permute-done.1.packed), custom_call_target="tpu_custom_call" | custom-call | flops 1000000000 | bytes 4000000 | tf_op jit(solution)/shard_map/pallas_call | solution.py:439
  69.3 0.9 copy-done.5
  70.2 2.7 %collective-permute-start.3 = (f32[256,256]{1,0:T(8,128)S(1)}, f32[256,256]{1,0:T(8,128)S(1)}, u32[]{:S(2)}, u32[]{:S(2)}) collective-permute-start(f32[256,256]{1,0:T(8,128)S(1)} %get-tuple-element.42.part_in), channel_id=1, source_target_pairs={{0,1},{1,0},{2,3},{3,2},{4,5},{5,4},{6,7},{7,6},{8,9},{9,8},{10,11... | collective-permute-start | bytes 786440 | tf_op jit(solution)/shard_map/ppermute | solution.py:21
  72.9 1.1 collective-permute-done.3.part_got
  74.0 3.2 %shard_map.117 = (bf16[1024,256]{1,0:T(8,128)(2,1)}, bf16[256,256]{1,0:T(8,128)(2,1)}) custom-call(f32[256,256]{1,0:T(8,128)S(1)} %get-tuple-element.42.part_in, f32[256,256]{1,0:T(8,128)S(1)} %collective-permute-done.3.part_got, f32[512,128]{1,0:T(8,128)S(1)} %copy-done.9, f32[512,128]{1,0:T(8,128)S(1)} %collective-permute-done.2.acts_got, ...), custom_call_target="tpu_custom_call" | custom-call | flops 1000000000 | bytes 4000000 | tf_op jit(solution)/shard_map/pallas_call | solution.py:457
  77.3 7.2 %all-to-all-start.1 = ((bf16[64,16,256]{2,1,0:T(8,128)(2,1)}), bf16[64,16,256]{2,1,0:T(8,128)(2,1)S(1)}, u32[]{:S(2)}, u32[]{:S(2)}) async-start(bf16[64,16,256]{2,1,0:T(8,128)(2,1)} %bitcast.28), calls=%async_computation.1 | async-start | bytes 1048576 | tf_op jit(solution)/shard_map/all_to_all | solution.py:44
  84.5 2.6 %collective-permute-start.5 = (bf16[1536,256]{1,0:T(8,128)(2,1)}, bf16[1536,256]{1,0:T(8,128)(2,1)}, u32[]{:S(2)}, u32[]{:S(2)}) collective-permute-start(bf16[1536,256]{1,0:T(8,128)(2,1)} %bitcast.24), channel_id=1, source_target_pairs={{0,1},{1,0},{2,3},{3,2},{4,5},{5,4},{6,7},{7,6},{8,9},{9,8},{10,11... | collective-permute-start | bytes 2359304 | tf_op jit(solution)/shard_map/ppermute | solution.py:21
  87.1 1.9 %collective-permute-start.4 = (bf16[32,2,2048]{2,1,0:T(2,128)(2,1)}, bf16[32,2,2048]{2,1,0:T(2,128)(2,1)}, u32[]{:S(2)}, u32[]{:S(2)}) collective-permute-start(bf16[32,2,2048]{2,1,0:T(2,128)(2,1)} %collective-permute-done), channel_id=1, source_target_pairs={{0,1},{1,0},{2,3},{3,2},{4,5},{5,4},{6,7},{7,6},{8,9},{9,8},{10,11... | collective-permute-start | bytes 786440 | tf_op jit(solution)/shard_map/ppermute | solution.py:21
  89.1 1.0 reshape.32.x_own
  90.9 1.8 %reshape.33.x_other = bf16[64,2048]{1,0:T(8,128)(2,1)} reshape(bf16[32,2,2048]{2,1,0:T(2,128)(2,1)} %collective-permute-done.4) | data formatting | bytes 524288 | tf_op jit(solution)/shard_map/reshape | solution.py:491
  92.7 0.9 copy-done.4
  93.6 1.1 copy-done.6
  95.6 4.1 %shard_map.118 = (bf16[2,2048,128]{2,1,0:T(8,128)(2,1)}, bf16[128,2048]{1,0:T(8,128)(2,1)}) custom-call(s32[64]{0:T(128)S(1)} %copy-done.13, bf16[256,2048]{1,0:T(8,128)(2,1)S(1)} %copy-done.1, bf16[64,2048]{1,0:T(8,128)(2,1)S(1)} %reshape.32.x_own, bf16[64,2048]{1,0:T(8,128)(2,1)S(1)} %copy-done.4, bf16[384,1024]{1,0:T(8,128)(2,1)S(1)} %copy-done.6, ...), custom_call_target="tpu_custom_call" | custom-call | flops 100000000 | bytes 1000000 | tf_op jit(solution)/shard_map/pallas_call | solution.py:479
  99.7 1.2 %all-to-all-done.1 = bf16[64,16,256]{2,1,0:T(8,128)(2,1)S(1)} async-done(((bf16[64,16,256]{2,1,0:T(8,128)(2,1)}), bf16[64,16,256]{2,1,0:T(8,128)(2,1)S(1)}, u32[]{:S(2)}, u32[]{:S(2)}) %all-to-all-start.1) | async-done | bytes 524320 | tf_op jit(solution)/shard_map/all_to_all | solution.py:44
  101.0 0.8 copy-done.12
  102.3 1.9 %collective-permute-start.7 = (bf16[16,1024]{1,0:T(8,128)(2,1)S(1)}, bf16[16,1024]{1,0:T(8,128)(2,1)S(1)}, u32[]{:S(2)}, u32[]{:S(2)}) collective-permute-start(bf16[16,1024]{1,0:T(8,128)(2,1)S(1)} %get-tuple-element.56), channel_id=1, source_target_pairs={{0,4},{1,5},{2,0},{3,1},{4,2},{5,3},{6,10},{7,11},{8,6},{9,7},{10,... | collective-permute-start | bytes 98312 | tf_op jit(solution)/shard_map/ppermute | solution.py:21
  104.2 3.4 %collective-permute-start.6 = (bf16[16,1024]{1,0:T(8,128)(2,1)S(1)}, bf16[16,1024]{1,0:T(8,128)(2,1)S(1)}, u32[]{:S(2)}, u32[]{:S(2)}) collective-permute-start(bf16[16,1024]{1,0:T(8,128)(2,1)S(1)} %get-tuple-element.56), channel_id=1, source_target_pairs={{0,2},{1,3},{2,4},{3,5},{4,0},{5,1},{6,8},{7,9},{8,10},{9,11},{10,... | collective-permute-start | bytes 98312 | tf_op jit(solution)/shard_map/ppermute | solution.py:21
  107.6 2.2 %collective-permute-done.6 = bf16[16,1024]{1,0:T(8,128)(2,1)S(1)} collective-permute-done((bf16[16,1024]{1,0:T(8,128)(2,1)S(1)}, bf16[16,1024]{1,0:T(8,128)(2,1)S(1)}, u32[]{:S(2)}, u32[]{:S(2)}) %collective-permute-start.6) | collective-permute-done | bytes 32800 | tf_op jit(solution)/shard_map/ppermute | solution.py:21
  109.8 3.9 %collective-permute-start.8 = (bf16[16,1024]{1,0:T(8,128)(2,1)S(1)}, bf16[16,1024]{1,0:T(8,128)(2,1)S(1)}, u32[]{:S(2)}, u32[]{:S(2)}) collective-permute-start(bf16[16,1024]{1,0:T(8,128)(2,1)S(1)} %fusion), channel_id=1, source_target_pairs={{0,6},{1,7},{2,8},{3,9},{4,10},{5,11},{6,0},{7,1},{8,2},{9,3},{10,... | collective-permute-start | bytes 98312 | tf_op jit(solution)/shard_map/ppermute | solution.py:21
  113.7 2.6 %collective-permute-done.8 = bf16[16,1024]{1,0:T(8,128)(2,1)S(1)} collective-permute-done((bf16[16,1024]{1,0:T(8,128)(2,1)S(1)}, bf16[16,1024]{1,0:T(8,128)(2,1)S(1)}, u32[]{:S(2)}, u32[]{:S(2)}) %collective-permute-start.8) | collective-permute-done | bytes 32800 | tf_op jit(solution)/shard_map/ppermute | solution.py:21
  116.3 5.2 %collective-permute-start.9 = (bf16[16,1024]{1,0:T(8,128)(2,1)S(1)}, bf16[16,1024]{1,0:T(8,128)(2,1)S(1)}, u32[]{:S(2)}, u32[]{:S(2)}) collective-permute-start(bf16[16,1024]{1,0:T(8,128)(2,1)S(1)} %add_convert_fusion.own), channel_id=1, source_target_pairs={{0,1},{1,0},{2,3},{3,2},{4,5},{5,4},{6,7},{7,6},{8,9},{9,8},{10,11... | collective-permute-start | bytes 98312 | tf_op jit(solution)/shard_map/ppermute | solution.py:21
  (36 shorter events, 3.7 us)
Async XLA Ops:
  2.3 48.6 %collective-permute-start = (bf16[32,2,2048]{2,1,0:T(2,128)(2,1)}, bf16[32,2,2048]{2,1,0:T(2,128)(2,1)}, u32[]{:S(2)}, u32[]{:S(2)}) collective-permute-start(bf16[32,2,2048]{2,1,0:T(2,128)(2,1)} %shard_map.112), channel_id=1, source_target_pairs={{0,22},{1,23},{2,20},{3,21},{4,18},{5,19},{6,16},{7,17},{8,14},{9,... | collective-permute-start | bytes 786440 | tf_op jit(solution)/shard_map/ppermute | solution.py:37
  20.8 46.4 %all-to-all-start = ((bf16[64,24,256]{2,1,0:T(8,128)(2,1)}), bf16[64,24,256]{2,1,0:T(8,128)(2,1)S(1)}, u32[]{:S(2)}, u32[]{:S(2)}) async-start(bf16[64,24,256]{2,1,0:T(8,128)(2,1)} %bitcast.27), calls=%async_computation | async-start | bytes 1572864 | tf_op jit(solution)/shard_map/all_to_all | solution.py:44
  30.4 5.9 %copy-start.14 = (bf16[1,2,64,2,2048]{4,3,2,1,0:T(2,128)(2,1)S(1)}, bf16[1,2,64,2,2048]{4,3,2,1,0:T(2,128)(2,1)}, u32[]{:S(2)}) copy-start(bf16[1,2,64,2,2048]{4,3,2,1,0:T(2,128)(2,1)} %saved.1) | copy-start | bytes 3145732
  33.2 17.8 %collective-permute-start.1 = (bf16[6144,128]{1,0:T(8,128)(2,1)}, bf16[6144,128]{1,0:T(8,128)(2,1)}, u32[]{:S(2)}, u32[]{:S(2)}) collective-permute-start(bf16[6144,128]{1,0:T(8,128)(2,1)} %shard_map.115), channel_id=1, source_target_pairs={{0,1},{1,0},{2,3},{3,2},{4,5},{5,4},{6,7},{7,6},{8,9},{9,8},{10,11... | collective-permute-start | bytes 4718600 | tf_op jit(solution)/shard_map/ppermute | solution.py:21
  37.6 29.7 %copy-start.3 = (bf16[1,128,2048]{2,1,0:T(8,128)(2,1)S(1)}, bf16[1,128,2048]{2,1,0:T(8,128)(2,1)}, u32[]{:S(2)}) copy-start(bf16[1,128,2048]{2,1,0:T(8,128)(2,1)} %param.15) | copy-start | bytes 1572868
  37.6 29.7 %copy-start.8 = (bf16[1,128,2048]{2,1,0:T(8,128)(2,1)S(1)}, bf16[1,128,2048]{2,1,0:T(8,128)(2,1)}, u32[]{:S(2)}) copy-start(bf16[1,128,2048]{2,1,0:T(8,128)(2,1)} %param.17) | copy-start | bytes 1572868
  41.0 10.0 %collective-permute-start.2 = (f32[512,128]{1,0:T(8,128)}, f32[512,128]{1,0:T(8,128)S(1)}, u32[]{:S(2)}, u32[]{:S(2)}) collective-permute-start(f32[512,128]{1,0:T(8,128)} %get-tuple-element.43.acts_in), channel_id=1, source_target_pairs={{0,1},{1,0},{2,3},{3,2},{4,5},{5,4},{6,7},{7,6},{8,9},{9,8},{10,11... | collective-permute-start | bytes 786440 | tf_op jit(solution)/shard_map/ppermute | solution.py:21
  67.2 2.1 %copy-start.7 = (bf16[64,24,256]{2,1,0:T(8,128)(2,1)}, bf16[64,24,256]{2,1,0:T(8,128)(2,1)S(1)}, u32[]{:S(2)}) copy-start(bf16[64,24,256]{2,1,0:T(8,128)(2,1)S(1)} %all-to-all-done) | copy-start | bytes 2359300
  67.2 6.8 %copy-start = (bf16[1,2,2048,128]{3,2,1,0:T(8,128)(2,1)S(1)}, bf16[1,2,2048,128]{3,2,1,0:T(8,128)(2,1)}, u32[]{:S(2)}) copy-start(bf16[1,2,2048,128]{3,2,1,0:T(8,128)(2,1)} %param.14) | copy-start | bytes 3145732
  67.2 6.8 %copy-start.2 = (bf16[1,2,2048,128]{3,2,1,0:T(8,128)(2,1)S(1)}, bf16[1,2,2048,128]{3,2,1,0:T(8,128)(2,1)}, u32[]{:S(2)}) copy-start(bf16[1,2,2048,128]{3,2,1,0:T(8,128)(2,1)} %param.16) | copy-start | bytes 3145732
  67.3 6.8 %copy-start.9 = (f32[512,128]{1,0:T(8,128)S(1)}, f32[512,128]{1,0:T(8,128)}, u32[]{:S(2)}) copy-start(f32[512,128]{1,0:T(8,128)} %get-tuple-element.43.acts_in) | copy-start | bytes 786436
  69.3 0.9 copy-start.5
  70.2 3.8 %collective-permute-start.3 = (f32[256,256]{1,0:T(8,128)S(1)}, f32[256,256]{1,0:T(8,128)S(1)}, u32[]{:S(2)}, u32[]{:S(2)}) collective-permute-start(f32[256,256]{1,0:T(8,128)S(1)} %get-tuple-element.42.part_in), channel_id=1, source_target_pairs={{0,1},{1,0},{2,3},{3,2},{4,5},{5,4},{6,7},{7,6},{8,9},{9,8},{10,11... | collective-permute-start | bytes 786440 | tf_op jit(solution)/shard_map/ppermute | solution.py:21
  77.3 15.4 %copy-start.1 = (bf16[256,2048]{1,0:T(8,128)(2,1)S(1)}, bf16[256,2048]{1,0:T(8,128)(2,1)}, u32[]{:S(2)}) copy-start(bf16[256,2048]{1,0:T(8,128)(2,1)} %reshape.29.x) | copy-start | bytes 3145732
  77.3 15.4 %copy-start.10 = (bf16[256,256]{1,0:T(8,128)(2,1)S(1)}, bf16[256,256]{1,0:T(8,128)(2,1)}, u32[]{:S(2)}) copy-start(bf16[256,256]{1,0:T(8,128)(2,1)} %get-tuple-element.50.grads) | copy-start | bytes 393220
  77.3 15.4 %copy-start.13 = (s32[64]{0:T(128)S(1)}, s32[64]{0:T(128)}, u32[]{:S(2)}) copy-start(s32[64]{0:T(128)} %experts.1) | copy-start | bytes 772
  77.3 23.7 %all-to-all-start.1 = ((bf16[64,16,256]{2,1,0:T(8,128)(2,1)}), bf16[64,16,256]{2,1,0:T(8,128)(2,1)S(1)}, u32[]{:S(2)}, u32[]{:S(2)}) async-start(bf16[64,16,256]{2,1,0:T(8,128)(2,1)} %bitcast.28), calls=%async_computation.1 | async-start | bytes 1048576 | tf_op jit(solution)/shard_map/all_to_all | solution.py:44
  84.5 8.1 %collective-permute-start.5 = (bf16[1536,256]{1,0:T(8,128)(2,1)}, bf16[1536,256]{1,0:T(8,128)(2,1)}, u32[]{:S(2)}, u32[]{:S(2)}) collective-permute-start(bf16[1536,256]{1,0:T(8,128)(2,1)} %bitcast.24), channel_id=1, source_target_pairs={{0,1},{1,0},{2,3},{3,2},{4,5},{5,4},{6,7},{7,6},{8,9},{9,8},{10,11... | collective-permute-start | bytes 2359304 | tf_op jit(solution)/shard_map/ppermute | solution.py:21
  87.1 3.8 %collective-permute-start.4 = (bf16[32,2,2048]{2,1,0:T(2,128)(2,1)}, bf16[32,2,2048]{2,1,0:T(2,128)(2,1)}, u32[]{:S(2)}, u32[]{:S(2)}) collective-permute-start(bf16[32,2,2048]{2,1,0:T(2,128)(2,1)} %collective-permute-done), channel_id=1, source_target_pairs={{0,1},{1,0},{2,3},{3,2},{4,5},{5,4},{6,7},{7,6},{8,9},{9,8},{10,11... | collective-permute-start | bytes 786440 | tf_op jit(solution)/shard_map/ppermute | solution.py:21
  92.7 1.0 copy-start.4
  93.6 1.1 copy-start.6
  94.8 0.8 copy-start.11
  101.0 0.8 copy-start.12
  102.3 5.3 %collective-permute-start.7 = (bf16[16,1024]{1,0:T(8,128)(2,1)S(1)}, bf16[16,1024]{1,0:T(8,128)(2,1)S(1)}, u32[]{:S(2)}, u32[]{:S(2)}) collective-permute-start(bf16[16,1024]{1,0:T(8,128)(2,1)S(1)} %get-tuple-element.56), channel_id=1, source_target_pairs={{0,4},{1,5},{2,0},{3,1},{4,2},{5,3},{6,10},{7,11},{8,6},{9,7},{10,... | collective-permute-start | bytes 98312 | tf_op jit(solution)/shard_map/ppermute | solution.py:21
  104.2 5.6 %collective-permute-start.6 = (bf16[16,1024]{1,0:T(8,128)(2,1)S(1)}, bf16[16,1024]{1,0:T(8,128)(2,1)S(1)}, u32[]{:S(2)}, u32[]{:S(2)}) collective-permute-start(bf16[16,1024]{1,0:T(8,128)(2,1)S(1)} %get-tuple-element.56), channel_id=1, source_target_pairs={{0,2},{1,3},{2,4},{3,5},{4,0},{5,1},{6,8},{7,9},{8,10},{9,11},{10,... | collective-permute-start | bytes 98312 | tf_op jit(solution)/shard_map/ppermute | solution.py:21
  109.8 6.5 %collective-permute-start.8 = (bf16[16,1024]{1,0:T(8,128)(2,1)S(1)}, bf16[16,1024]{1,0:T(8,128)(2,1)S(1)}, u32[]{:S(2)}, u32[]{:S(2)}) collective-permute-start(bf16[16,1024]{1,0:T(8,128)(2,1)S(1)} %fusion), channel_id=1, source_target_pairs={{0,6},{1,7},{2,8},{3,9},{4,10},{5,11},{6,0},{7,1},{8,2},{9,3},{10,... | collective-permute-start | bytes 98312 | tf_op jit(solution)/shard_map/ppermute | solution.py:21
  116.3 6.1 %collective-permute-start.9 = (bf16[16,1024]{1,0:T(8,128)(2,1)S(1)}, bf16[16,1024]{1,0:T(8,128)(2,1)S(1)}, u32[]{:S(2)}, u32[]{:S(2)}) collective-permute-start(bf16[16,1024]{1,0:T(8,128)(2,1)S(1)} %add_convert_fusion.own), channel_id=1, source_target_pairs={{0,1},{1,0},{2,3},{3,2},{4,5},{5,4},{6,7},{7,6},{8,9},{9,8},{10,11... | collective-permute-start | bytes 98312 | tf_op jit(solution)/shard_map/ppermute | solution.py:21
